TPU v7x, 32 devices: a whole 2x2x4 slice. The times are simulated.
32 devices in a mesh: dp: 4 (over y, x), fsdp: 8 (over z, core).
Axes of the slice: x: 2, y: 2, z: 4, core: 2. Of those that a mesh axis runs over, the one named last changes fastest.
Arguments:
- short_tokens: bfloat16 [32, 512, 768], P(('dp', 'fsdp')), may hold values from -6 to 6
- long_tokens: bfloat16 [32, 1024, 768], P(('dp', 'fsdp')), may hold values from -6 to 6
- short_split: int32 [32], P(('dp', 'fsdp')), may hold values from 128 to 384, as said below
- long_split: int32 [32], P(('dp', 'fsdp')), may hold values from 256 to 768, as said below
- ln1_gain: bfloat16 [768], P(('dp', 'fsdp')), may hold values from 0.25 to 1.75
- ln1_bias: bfloat16 [768], P(('dp', 'fsdp')), may hold values from -4 to 4
- qkv_weight: bfloat16 [768, 2304], P(('dp', 'fsdp')), may hold values from -0.3125 to 0.3125
- qv_bias: bfloat16 [1536], P(('dp', 'fsdp')), may hold values from -4 to 4
- proj_weight: bfloat16 [768, 768], P(('dp', 'fsdp')), may hold values from -4 to 4
- proj_bias: bfloat16 [768], P(('dp', 'fsdp')), may hold values from -6 to 6
- ln2_gain: bfloat16 [768], P(('dp', 'fsdp')), may hold values from 0.25 to 1.75
- ln2_bias: bfloat16 [768], P(('dp', 'fsdp')), may hold values from -4 to 4
- fc_weight: bfloat16 [768, 3072], P(('dp', 'fsdp')), may hold values from -0.21875 to 0.21875
- fc_bias: bfloat16 [3072], P(('dp', 'fsdp')), may hold values from -4 to 4
- out_weight: bfloat16 [3072, 768], P(('dp', 'fsdp')), may hold values from -0.75 to 0.75
- out_bias: bfloat16 [768], P(('dp', 'fsdp')), may hold values from -6 to 6
- short_cotangent: bfloat16 [32, 512, 768], P(('dp', 'fsdp')), may hold values from -24 to 24
- long_cotangent: bfloat16 [32, 1024, 768], P(('dp', 'fsdp')), may hold values from -24 to 24
Outputs:
- short_output: bfloat16 [32, 512, 768], P(('dp', 'fsdp'))
- long_output: bfloat16 [32, 1024, 768], P(('dp', 'fsdp'))
- short_input_grad: float32 [32, 512, 768], P(('dp', 'fsdp'))
- long_input_grad: float32 [32, 1024, 768], P(('dp', 'fsdp'))
- ln1_gain_grad: float32 [768], P(('dp', 'fsdp'))
- ln1_bias_grad: float32 [768], P(('dp', 'fsdp'))
- qkv_weight_grad: float32 [768, 2304], P(('dp', 'fsdp'))
- qv_bias_grad: float32 [1536], P(('dp', 'fsdp'))
- proj_weight_grad: float32 [768, 768], P(('dp', 'fsdp'))
- proj_bias_grad: float32 [768], P(('dp', 'fsdp'))
- ln2_gain_grad: float32 [768], P(('dp', 'fsdp'))
- ln2_bias_grad: float32 [768], P(('dp', 'fsdp'))
- fc_weight_grad: float32 [768, 3072], P(('dp', 'fsdp'))
- fc_bias_grad: float32 [3072], P(('dp', 'fsdp'))
- out_weight_grad: float32 [3072, 768], P(('dp', 'fsdp'))
- out_bias_grad: float32 [768], P(('dp', 'fsdp'))
Inputs may be any that keep to these rules, and one draw needn't show every extreme that they name: `short_split`: each short sequence packs two documents, the first ending here; some sequence takes each end of the range. `long_split`: each long sequence packs two documents, the first ending here; some sequence takes each end of the range.
All inputs are finite; a program needn't handle non-finite values.
Results may differ from a plain program's by a relative error of at most 0.013.
The roundings to bfloat16 on the way count: a program that leaves them out, or rounds other values in their place, can miss the bound.
Values may be sent and summed in bfloat16 or wider, within the bound.
A program may use at most 320 MiB of HBM per device.

v0:
```python
import jax
import jax.numpy as jnp
from jax import lax
from jax.sharding import PartitionSpec as P

HEAD_DIM = 64


branch_scale = 0.14433756729740643
ln_epsilon = 1e-05
neg_large = -1e30


def layer_norm(values, norm_gain, norm_shift):
    center = values - jnp.mean(values, axis=-1, keepdims=True)
    spread = jnp.mean(center * center, axis=-1, keepdims=True)
    return center * lax.rsqrt(spread + ln_epsilon) * norm_gain + norm_shift


def gelu_tanh(values):
    return jax.nn.gelu(values, approximate=True)


def matmul(left, right):
    return jnp.dot(left, right, preferred_element_type=jnp.float32)


def matmul_tn(left, right):
    return lax.dot_general(
        left, right, (((0,), (0,)), ((), ())), preferred_element_type=jnp.float32
    )


def matmul_nt(left, right):
    return lax.dot_general(
        left, right, (((1,), (1,)), ((), ())), preferred_element_type=jnp.float32
    )


def visible_mask(query_pos, key_pos, split_at):
    causal = key_pos[None, :] <= query_pos[:, None]
    same_doc = (key_pos[None, :] >= split_at) == (query_pos[:, None] >= split_at)
    return causal & same_doc


def attend_forward(queries, keys_in, values_in, split_at):
    length, head_count, head_width = queries.shape
    rows_block = min(512, length)
    half_heads = head_count // 2
    scale_factor = head_width ** (-0.5)
    positions = jnp.arange(length, dtype=jnp.int32)
    attended_rows = []
    total_rows = []
    for row_start in range(0, length, rows_block):
        row_stop = row_start + rows_block
        allowed = visible_mask(positions[row_start:row_stop], positions[:row_stop], split_at)
        head_outs = []
        head_totals = []
        for head_start in (0, half_heads):
            head_stop = head_start + half_heads
            scores = (
                jnp.einsum(
                    "qhd,khd->hqk",
                    queries[row_start:row_stop, head_start:head_stop],
                    keys_in[:row_stop, head_start:head_stop],
                    preferred_element_type=jnp.float32,
                )
                * scale_factor
            )
            scores = jnp.where(allowed[None], scores, neg_large)
            row_peak = jnp.max(scores, axis=-1, keepdims=True)
            exponent = jnp.exp(scores - row_peak)
            totals = jnp.sum(exponent, axis=-1, keepdims=True)
            prob_low = (exponent / totals).astype(jnp.bfloat16)
            head_outs.append(
                jnp.einsum(
                    "hqk,khd->qhd",
                    prob_low,
                    values_in[:row_stop, head_start:head_stop],
                    preferred_element_type=jnp.float32,
                )
            )
            head_totals.append((row_peak + jnp.log(totals))[..., 0])
        attended_rows.append(jnp.concatenate(head_outs, axis=1))
        total_rows.append(jnp.concatenate(head_totals, axis=0))
    attended = jnp.concatenate(attended_rows, axis=0).astype(jnp.bfloat16)
    return (attended, jnp.concatenate(total_rows, axis=1))


def attend_backward(queries, keys_in, values_in, split_at, log_totals, grad_attended):
    length, head_count, head_width = queries.shape
    rows_block = min(512, length)
    half_heads = head_count // 2
    scale_factor = head_width ** (-0.5)
    positions = jnp.arange(length, dtype=jnp.int32)
    grad_query = jnp.zeros(queries.shape, jnp.float32)
    grad_key = jnp.zeros(queries.shape, jnp.float32)
    grad_value = jnp.zeros(queries.shape, jnp.float32)
    for row_start in range(0, length, rows_block):
        row_stop = row_start + rows_block
        allowed = visible_mask(positions[row_start:row_stop], positions[:row_stop], split_at)
        for head_start in (0, half_heads):
            head_stop = head_start + half_heads
            query_part = queries[row_start:row_stop, head_start:head_stop]
            key_part = keys_in[:row_stop, head_start:head_stop]
            value_part = values_in[:row_stop, head_start:head_stop]
            grad_part = grad_attended[row_start:row_stop, head_start:head_stop]
            scores = (
                jnp.einsum("qhd,khd->hqk", query_part, key_part, preferred_element_type=jnp.float32)
                * scale_factor
            )
            scores = jnp.where(allowed[None], scores, neg_large)
            probs = jnp.exp(
                scores - log_totals[head_start:head_stop, row_start:row_stop][..., None]
            )
            grad_probs = jnp.einsum(
                "qhd,khd->hqk", grad_part, value_part, preferred_element_type=jnp.float32
            )
            grad_value = grad_value.at[:row_stop, head_start:head_stop].add(
                jnp.einsum(
                    "hqk,qhd->khd",
                    probs.astype(jnp.bfloat16),
                    grad_part,
                    preferred_element_type=jnp.float32,
                )
            )
            inner = jnp.sum(probs * grad_probs, axis=-1, keepdims=True)
            grad_scores = (probs * (grad_probs - inner)).astype(jnp.bfloat16)
            grad_query = grad_query.at[row_start:row_stop, head_start:head_stop].add(
                jnp.einsum(
                    "hqk,khd->qhd", grad_scores, key_part, preferred_element_type=jnp.float32
                )
                * scale_factor
            )
            grad_key = grad_key.at[:row_stop, head_start:head_stop].add(
                jnp.einsum(
                    "hqk,qhd->khd", grad_scores, query_part, preferred_element_type=jnp.float32
                )
                * scale_factor
            )
    return jnp.stack((grad_query, grad_key, grad_value), axis=1)


def attention_group(tokens, splits, attention_params):
    gain_one, shift_one, qkv_weights, qv_shift, proj_weights, proj_shift = attention_params
    seq_count, length, model_width = tokens.shape
    inputs = tokens.reshape(seq_count * length, model_width).astype(jnp.float32)
    norm_one = layer_norm(
        inputs, gain_one.astype(jnp.float32), shift_one.astype(jnp.float32)
    ).astype(jnp.bfloat16)
    qv_float = qv_shift.astype(jnp.float32)
    shift_full = jnp.concatenate(
        [qv_float[:model_width], jnp.zeros((model_width,), jnp.float32), qv_float[model_width:]]
    )
    mixed = (matmul(norm_one, qkv_weights) + shift_full).astype(jnp.bfloat16)
    split_qkv = mixed.reshape(seq_count, length, 3, model_width // HEAD_DIM, HEAD_DIM)
    attended, log_totals = lax.map(
        lambda seq_item: attend_forward(
            seq_item[0][:, 0], seq_item[0][:, 1], seq_item[0][:, 2], seq_item[1]
        ),
        (split_qkv, splits),
    )
    attended = attended.reshape(seq_count * length, model_width)
    attn_out = matmul(attended, proj_weights) + proj_shift.astype(jnp.float32)
    middle = inputs + branch_scale * attn_out
    return (inputs, norm_one, split_qkv, attended, log_totals, middle)


def mlp_group(middle, mlp_params):
    gain_two, shift_two, fc_weights, fc_shift, out_weights, out_shift = mlp_params
    norm_two = layer_norm(
        middle, gain_two.astype(jnp.float32), shift_two.astype(jnp.float32)
    ).astype(jnp.bfloat16)
    pre_act = matmul(norm_two, fc_weights) + fc_shift.astype(jnp.float32)
    activated = gelu_tanh(pre_act).astype(jnp.bfloat16)
    mlp_out = matmul(activated, out_weights) + out_shift.astype(jnp.float32)
    return (norm_two, pre_act, activated, middle + branch_scale * mlp_out)


def mlp_backward(grad_out, middle, mlp_saved, mlp_params):
    gain_two, shift_two, fc_weights, fc_shift, out_weights, out_shift = mlp_params
    norm_two, pre_act, activated, result = mlp_saved
    grad_mlp = (branch_scale * grad_out).astype(jnp.bfloat16)
    out_weight_grad = matmul_tn(activated, grad_mlp)
    out_shift_grad = jnp.sum(grad_mlp.astype(jnp.float32), axis=0)
    grad_act = matmul_nt(grad_mlp, out_weights)
    unused_value, gelu_pull = jax.vjp(gelu_tanh, pre_act)
    grad_pre = gelu_pull(grad_act)[0].astype(jnp.bfloat16)
    fc_weight_grad = matmul_tn(norm_two, grad_pre)
    fc_shift_grad = jnp.sum(grad_pre.astype(jnp.float32), axis=0)
    grad_norm = matmul_nt(grad_pre, fc_weights)
    unused_norm, norm_pull = jax.vjp(
        layer_norm, middle, gain_two.astype(jnp.float32), shift_two.astype(jnp.float32)
    )
    grad_middle, gain_grad, shift_grad = norm_pull(grad_norm)
    return (
        grad_out + grad_middle,
        (gain_grad, shift_grad, fc_weight_grad, fc_shift_grad, out_weight_grad, out_shift_grad),
    )


def attention_backward(grad_middle, splits, attention_saved, attention_params):
    gain_one, shift_one, qkv_weights, qv_shift, proj_weights, proj_shift = attention_params
    inputs, norm_one, split_qkv, attended, log_totals, middle = attention_saved
    seq_count, length = (split_qkv.shape[0], split_qkv.shape[1])
    model_width = inputs.shape[1]
    grad_attn = (branch_scale * grad_middle).astype(jnp.bfloat16)
    proj_weight_grad = matmul_tn(attended, grad_attn)
    proj_shift_grad = jnp.sum(grad_attn.astype(jnp.float32), axis=0)
    grad_attended = matmul_nt(grad_attn, proj_weights).astype(jnp.bfloat16)
    grad_attended = grad_attended.reshape(seq_count, length, model_width // HEAD_DIM, HEAD_DIM)
    grad_qkv = lax.map(
        lambda seq_item: attend_backward(
            seq_item[0][:, 0],
            seq_item[0][:, 1],
            seq_item[0][:, 2],
            seq_item[1],
            seq_item[2],
            seq_item[3],
        ),
        (split_qkv, splits, log_totals, grad_attended),
    )
    grad_qkv = grad_qkv.reshape(seq_count * length, 3 * model_width).astype(jnp.bfloat16)
    qkv_weight_grad = matmul_tn(norm_one, grad_qkv)
    column_sums = jnp.sum(grad_qkv.astype(jnp.float32), axis=0)
    qv_shift_grad = jnp.concatenate([column_sums[:model_width], column_sums[2 * model_width :]])
    grad_norm = matmul_nt(grad_qkv, qkv_weights)
    unused_norm, norm_pull = jax.vjp(
        layer_norm, inputs, gain_one.astype(jnp.float32), shift_one.astype(jnp.float32)
    )
    grad_inputs, gain_grad, shift_grad = norm_pull(grad_norm)
    return (
        grad_middle + grad_inputs,
        (gain_grad, shift_grad, qkv_weight_grad, qv_shift_grad, proj_weight_grad, proj_shift_grad),
    )


def per_device(
    short_tokens,
    long_tokens,
    short_split,
    long_split,
    ln1_gain,
    ln1_bias,
    qkv_weight,
    qv_bias,
    proj_weight,
    proj_bias,
    ln2_gain,
    ln2_bias,
    fc_weight,
    fc_bias,
    out_weight,
    out_bias,
    short_cotangent,
    long_cotangent,
):
    attention_full = (
        lax.all_gather(ln1_gain, ("dp", "fsdp"), axis=0, tiled=True),
        lax.all_gather(ln1_bias, ("dp", "fsdp"), axis=0, tiled=True),
        lax.all_gather(qkv_weight, ("dp", "fsdp"), axis=0, tiled=True),
        lax.all_gather(qv_bias, ("dp", "fsdp"), axis=0, tiled=True),
        lax.all_gather(proj_weight, ("dp", "fsdp"), axis=0, tiled=True),
        lax.all_gather(proj_bias, ("dp", "fsdp"), axis=0, tiled=True),
    )
    short_attention = attention_group(short_tokens, short_split, attention_full)
    long_attention = attention_group(long_tokens, long_split, attention_full)
    mlp_full = (
        lax.all_gather(ln2_gain, ("dp", "fsdp"), axis=0, tiled=True),
        lax.all_gather(ln2_bias, ("dp", "fsdp"), axis=0, tiled=True),
        lax.all_gather(fc_weight, ("dp", "fsdp"), axis=0, tiled=True),
        lax.all_gather(fc_bias, ("dp", "fsdp"), axis=0, tiled=True),
        lax.all_gather(out_weight, ("dp", "fsdp"), axis=0, tiled=True),
        lax.all_gather(out_bias, ("dp", "fsdp"), axis=0, tiled=True),
    )
    short_mlp = mlp_group(short_attention[5], mlp_full)
    long_mlp = mlp_group(long_attention[5], mlp_full)
    mlp_back = (
        lax.all_gather(ln2_gain, ("dp", "fsdp"), axis=0, tiled=True),
        lax.all_gather(ln2_bias, ("dp", "fsdp"), axis=0, tiled=True),
        lax.all_gather(fc_weight, ("dp", "fsdp"), axis=0, tiled=True),
        lax.all_gather(fc_bias, ("dp", "fsdp"), axis=0, tiled=True),
        lax.all_gather(out_weight, ("dp", "fsdp"), axis=0, tiled=True),
        lax.all_gather(out_bias, ("dp", "fsdp"), axis=0, tiled=True),
    )
    short_grad_out = short_cotangent.reshape(short_attention[0].shape).astype(jnp.float32)
    long_grad_out = long_cotangent.reshape(long_attention[0].shape).astype(jnp.float32)
    short_grad_mid, short_mlp_terms = mlp_backward(
        short_grad_out, short_attention[5], short_mlp, mlp_back
    )
    long_grad_mid, long_mlp_terms = mlp_backward(
        long_grad_out, long_attention[5], long_mlp, mlp_back
    )
    mlp_totals = jax.tree.map(jnp.add, short_mlp_terms, long_mlp_terms)
    mlp_shares = (
        lax.psum_scatter(mlp_totals[0], ("dp", "fsdp"), scatter_dimension=0, tiled=True),
        lax.psum_scatter(mlp_totals[1], ("dp", "fsdp"), scatter_dimension=0, tiled=True),
        lax.psum_scatter(mlp_totals[2], ("dp", "fsdp"), scatter_dimension=0, tiled=True),
        lax.psum_scatter(mlp_totals[3], ("dp", "fsdp"), scatter_dimension=0, tiled=True),
        lax.psum_scatter(mlp_totals[4], ("dp", "fsdp"), scatter_dimension=0, tiled=True),
        lax.psum_scatter(mlp_totals[5], ("dp", "fsdp"), scatter_dimension=0, tiled=True),
    )
    attention_back = (
        lax.all_gather(ln1_gain, ("dp", "fsdp"), axis=0, tiled=True),
        lax.all_gather(ln1_bias, ("dp", "fsdp"), axis=0, tiled=True),
        lax.all_gather(qkv_weight, ("dp", "fsdp"), axis=0, tiled=True),
        lax.all_gather(qv_bias, ("dp", "fsdp"), axis=0, tiled=True),
        lax.all_gather(proj_weight, ("dp", "fsdp"), axis=0, tiled=True),
        lax.all_gather(proj_bias, ("dp", "fsdp"), axis=0, tiled=True),
    )
    short_grad_in, short_attention_terms = attention_backward(
        short_grad_mid, short_split, short_attention, attention_back
    )
    long_grad_in, long_attention_terms = attention_backward(
        long_grad_mid, long_split, long_attention, attention_back
    )
    attention_totals = jax.tree.map(jnp.add, short_attention_terms, long_attention_terms)
    attention_shares = (
        lax.psum_scatter(attention_totals[0], ("dp", "fsdp"), scatter_dimension=0, tiled=True),
        lax.psum_scatter(attention_totals[1], ("dp", "fsdp"), scatter_dimension=0, tiled=True),
        lax.psum_scatter(attention_totals[2], ("dp", "fsdp"), scatter_dimension=0, tiled=True),
        lax.psum_scatter(attention_totals[3], ("dp", "fsdp"), scatter_dimension=0, tiled=True),
        lax.psum_scatter(attention_totals[4], ("dp", "fsdp"), scatter_dimension=0, tiled=True),
        lax.psum_scatter(attention_totals[5], ("dp", "fsdp"), scatter_dimension=0, tiled=True),
    )
    short_output = short_mlp[3].reshape(short_tokens.shape).astype(jnp.bfloat16)
    long_output = long_mlp[3].reshape(long_tokens.shape).astype(jnp.bfloat16)
    short_input_grad = short_grad_in.reshape(short_tokens.shape)
    long_input_grad = long_grad_in.reshape(long_tokens.shape)
    return (
        short_output,
        long_output,
        short_input_grad,
        long_input_grad,
        attention_shares[0],
        attention_shares[1],
        attention_shares[2],
        attention_shares[3],
        attention_shares[4],
        attention_shares[5],
        mlp_shares[0],
        mlp_shares[1],
        mlp_shares[2],
        mlp_shares[3],
        mlp_shares[4],
        mlp_shares[5],
    )


def solution(mesh):
    in_specs = (
        P(("dp", "fsdp"), None, None),
        P(("dp", "fsdp"), None, None),
        P(("dp", "fsdp")),
        P(("dp", "fsdp")),
        P(("dp", "fsdp")),
        P(("dp", "fsdp")),
        P(("dp", "fsdp"), None),
        P(("dp", "fsdp")),
        P(("dp", "fsdp"), None),
        P(("dp", "fsdp")),
        P(("dp", "fsdp")),
        P(("dp", "fsdp")),
        P(("dp", "fsdp"), None),
        P(("dp", "fsdp")),
        P(("dp", "fsdp"), None),
        P(("dp", "fsdp")),
        P(("dp", "fsdp"), None, None),
        P(("dp", "fsdp"), None, None),
    )
    out_specs = (
        P(("dp", "fsdp"), None, None),
        P(("dp", "fsdp"), None, None),
        P(("dp", "fsdp"), None, None),
        P(("dp", "fsdp"), None, None),
        P(("dp", "fsdp")),
        P(("dp", "fsdp")),
        P(("dp", "fsdp"), None),
        P(("dp", "fsdp")),
        P(("dp", "fsdp"), None),
        P(("dp", "fsdp")),
        P(("dp", "fsdp")),
        P(("dp", "fsdp")),
        P(("dp", "fsdp"), None),
        P(("dp", "fsdp")),
        P(("dp", "fsdp"), None),
        P(("dp", "fsdp")),
    )
    return jax.shard_map(
        per_device, mesh=mesh, in_specs=in_specs, out_specs=out_specs, check_vma=False
    )
```

profile of v0, /device:TPU:0, one launch (start us, length us, event | category | flops | bytes accessed | tf_op | source)
XLA Modules:
  0.0 914.5 jit_solution(6547846275562660766)
XLA Ops:
  21.6 42.9 %all-reduce.23 = (bf16[1536]{0:T(1024)(128)(2,1)S(1)}, bf16[768]{0:T(1024)(128)(2,1)S(1)}, bf16[768]{0:T(1024)(128)(2,1)S(1)}, bf16[768]{0:T(1024)(128)(2,1)S(1)...) all-reduce(bf16[1536]{0:T(1024)(128)(2,1)S(1)} %dynamic-update-slic, ...), channel_id=1, replica_groups=mesh['dp'=4,'fsdp'=8] {'dp','fsdp'}, use_global_device_ids=true, to_apply=%add.8 | all-reduce | flops 9216 | bytes 36864
  74.5 7.8 add_convert_fusion
  82.3 6.7 copy.99
  158.9 37.4 %all-gather.9.cloned.1.call-done = bf16[768,3072]{1,0:T(8,128)(2,1)} async-done(((bf16[24,3072]{1,0:T(8,128)(2,1)}), bf16[768,3072]{1,0:T(8,128)(2,1)}) %all-gather.9.cloned.1.call-update) | async-done | bytes 4718608 | tf_op jit(solution)/shard_map/all_gather | solution.py:271
  196.3 7.0 fusion.237
  203.4 58.3 %all-gather.11.cloned.1.call-done = bf16[3072,768]{1,0:T(8,128)(2,1)} async-done(((bf16[96,768]{1,0:T(8,128)(2,1)}), bf16[3072,768]{1,0:T(8,128)(2,1)}) %all-gather.11.cloned.1.call-update) | async-done | bytes 4718608 | tf_op jit(solution)/shard_map/all_gather | solution.py:273
  261.7 10.1 %convert_reduce_fusion.2 = (f32[3072]{0:T(1024)}, bf16[512,3072]{1,0:T(8,128)(2,1)S(1)}) fusion(f32[512,3072]{1,0:T(8,128)} %fusion.237, f32[3072]{0:T(1024)S(1)} %copy-done.139, bf16[3072,768]{1,0:T(8,128)(2,1)} %all-gather.11.cloned.1.call-done, bf16[1,512,768]{2,1,0:T(8,128)(2,1)S(1)} %copy-done.55), kind=kOutput, calls=%fused_computation.41 | convolution fusion | flops 2453271552 | bytes 14966784 | tf_op jit(solution)/shard_map/dot_general | solution.py:35
  297.2 7.8 fusion.239
  305.0 17.5 %convert_reduce_fusion = (f32[3072]{0:T(1024)}, bf16[1024,3072]{1,0:T(8,128)(2,1)}) fusion(f32[1024,3072]{1,0:T(8,128)S(1)} %fusion.239, f32[3072]{0:T(1024)S(1)} %copy-done.139, bf16[3072,768]{1,0:T(8,128)(2,1)} %all-gather.11.cloned.1.call-done, bf16[1,1024,768]{1,2,0:T(8,128)(2,1)S(1)} %copy-done.22), kind=kOutput, calls=%fused_computation.9 | convolution fusion | flops 4906546176 | bytes 25190400 | tf_op jit(solution)/shard_map/dot_general | solution.py:35
  322.6 10.4 %fusion.256 = (f32[768]{0:T(1024)}, f32[1024,768]{1,0:T(8,128)}) fusion(bf16[1024,3072]{1,0:T(8,128)(2,1)} %get-tuple-element.527, bf16[768,3072]{1,0:T(8,128)(2,1)} %all-gather.9.cloned.1.call-done), kind=kOutput, calls=%fused_computation.373 | convolution fusion | flops 4832623616 | bytes 14158848 | tf_op jit(solution)/shard_map/dot_general | solution.py:35
  370.3 5.5 fusion.143
  393.1 9.9 %multiply_reduce_fusion.1 = (f32[6,512]{1,0:T(8,128)S(1)}, f32[6,512,1024]{2,1,0:T(8,128)}) fusion(f32[6,512,1024]{2,1,0:T(8,128)} %copy-done.1, f32[6,512]{1,0:T(8,128)S(1)} %log_add_fusion.1, bf16[1024,12,64]{0,2,1:T(8,128)(2,1)} %get-tuple-element.475, bf16[1024,12,64]{0,2,1:T(8,128)(2,1)} %bitcast.352), kind=kOutput, calls=%fused_computation.14 | convolution fusion | flops 412087296 | bytes 26370048 | tf_op jit(solution)/shard_map/while/body/eval_jaxpr/qhd,khd->hqk/dot_general | solution.py:116
  402.9 6.2 scatter-add.91
  409.1 8.7 fusion.94
  422.0 10.7 %multiply_reduce_fusion = (f32[6,512]{1,0:T(8,128)S(1)}, f32[6,512,1024]{2,1,0:T(8,128)}) fusion(f32[6,512,1024]{2,1,0:T(8,128)} %copy-done, f32[6,512]{1,0:T(8,128)S(1)} %copy-done.84, bf16[1024,12,64]{0,2,1:T(8,128)(2,1)S(1)} %copy-done.30, bf16[1024,12,64]{0,2,1:T(8,128)(2,1)S(1)} %bitcast.354), kind=kOutput, calls=%fused_computation.11 | convolution fusion | flops 412087296 | bytes 26374144 | tf_op jit(solution)/shard_map/while/body/eval_jaxpr/qhd,khd->hqk/dot_general | solution.py:116
  442.4 6.2 scatter-add.77
  448.6 9.7 %multiply_convert_fusion.1 = bf16[6,512,1024]{2,1,0:T(8,128)(2,1)S(1)} fusion(f32[6,512,1024]{2,1,0:T(8,128)} %get-tuple-element.517, f32[6,512,1024]{2,1,0:T(8,128)} %copy-done.1, f32[6,512]{1,0:T(8,128)S(1)} %get-tuple-element.516, f32[6,512]{1,0:T(8,128)S(1)} %log_add_fusion.1), kind=kLoop, calls=%fused_computation.13 | loop fusion | flops 12582912 | bytes 31481856 | tf_op jit(solution)/shard_map/while/body/eval_jaxpr/convert_element_type | solution.py:128
  467.1 6.5 multiply_convert_fusion.5
  476.8 6.3 multiply_convert_fusion
  500.4 5.4 convolution_add_fusion
  506.4 12.5 %fusion.166 = f32[3072,768]{1,0:T(8,128)S(1)} fusion(bf16[1,1024,768]{1,2,0:T(8,128)(2,1)} %copy.110, f32[1024,3072]{1,0:T(8,128)} %copy-done.24, f32[3072]{0:T(1024)S(1)} %copy-done.140), kind=kOutput, calls=%fused_computation.250 | convolution fusion | flops 4865654784 | bytes 23605248 | tf_op jit(solution)/shard_map/dot_general | solution.py:29
  518.9 10.7 %convolution_add_fusion.1 = f32[3072,768]{1,0:T(8,128)} fusion(f32[3072,768]{1,0:T(8,128)S(1)} %fusion.166, bf16[1,512,768]{2,1,0:T(8,128)(2,1)S(1)} %copy-done.56, f32[512,3072]{1,0:T(8,128)} %fusion.237, f32[3072]{0:T(1024)S(1)} %copy-done.140), kind=kOutput, calls=%fused_computation.76 | convolution fusion | flops 2435186688 | bytes 25964544 | tf_op jit(solution)/shard_map/dot_general | solution.py:29
  530.3 9.3 %fusion.238 = f32[768,3072]{1,0:T(8,128)S(1)} fusion(bf16[1024,3072]{1,0:T(8,128)(2,1)} %get-tuple-element.527, f32[1024,768]{0,1:T(8,128)} %copy-done.6, f32[768]{0:T(1024)S(1)} %copy-done.73, f32[768]{0:T(1024)S(1)} %copy-done.67, f32[1024]{0:T(1024)S(1)} %copy-done.77, f32[1024]{0:T(1024)S(1)} %copy-done.75), kind=kOutput, calls=%fused_computation.355 | convolution fusion | flops 4835770368 | bytes 18888704 | tf_op jit(solution)/shard_map/dot_general | solution.py:29
  539.7 5.8 convolution_add_fusion.2
  546.3 12.2 %fusion.106 = bf16[1,1024,768]{1,2,0:T(8,128)(2,1)} fusion(f32[1024,768]{0,1:T(8,128)} %copy-done.6, f32[768]{0:T(1024)S(1)} %convert_element_type.283, bf16[3072,768]{1,0:T(8,128)(2,1)} %all-gather.11.cloned.1.call-done, f32[1024,3072]{1,0:T(8,128)} %copy-done.24, f32[3072]{0:T(1024)S(1)} %copy-done.140), kind=kOutput, calls=%fused_computation.197 | convolution fusion | flops 4866441216 | bytes 22035456 | tf_op jit(solution)/shard_map/dot_general | solution.py:25
  561.2 9.0 fusion.255
  574.2 5.2 fusion.240
  582.2 41.2 %all-reduce.22 = (f32[768]{0:T(1024)S(1)}, f32[768]{0:T(1024)S(1)}, f32[1536]{0:T(1024)S(1)}, f32[768]{0:T(1024)S(1)}, f32[768]{0:T(1024)S(1)}, /*index=5*/f32[7...) all-reduce(f32[768]{0:T(1024)S(1)} %add.526, ...), channel_id=2, replica_groups=mesh['dp'=4,'fsdp'=8] {'dp','fsdp'}, use_global_device_ids=true, to_apply=%region_37.38.clone | all-reduce | flops 9216 | bytes 73728
  626.8 6.4 add_bitcast_fusion
  641.5 9.5 %fusion.111 = bf16[1,512,768]{2,1,0:T(8,128)(2,1)} fusion(f32[512,768]{1,0:T(8,128)S(1)} %copy-done.19, bf16[3072,768]{1,0:T(8,128)(2,1)} %all-gather.11.cloned.1.call-done, f32[768]{0:T(1024)S(1)} %convert_element_type.283, f32[512,3072]{1,0:T(8,128)} %fusion.237, f32[3072]{0:T(1024)S(1)} %copy-done.140), kind=kOutput, calls=%fused_computation.199 | convolution fusion | flops 2433220608 | bytes 13384704 | tf_op jit(solution)/shard_map/dot_general | solution.py:25
  651.0 114.3 %reduce-scatter.11.cloned.1.call-done = f32[96,768]{1,0:T(8,128)} async-done(((f32[3072,768]{1,0:T(8,128)}), f32[96,768]{1,0:T(8,128)}) %reduce-scatter.11.cloned.1.call-update) | async-done | bytes 294928 | tf_op jit(solution)/shard_map/reduce_scatter | solution.py:300
  765.3 142.2 %reduce-scatter.9.cloned.1.call-done = f32[24,3072]{1,0:T(8,128)} async-done(((f32[768,3072]{1,0:T(8,128)}), f32[24,3072]{1,0:T(8,128)}) %reduce-scatter.9.cloned.1.call-update) | async-done | bytes 294928 | tf_op jit(solution)/shard_map/reduce_scatter | solution.py:298
  (557 shorter events, 237.5 us)
Async XLA Ops:
  7.2 58.2 %copy-start.64 = (bf16[1,1024,768]{2,1,0:T(8,128)(2,1)S(1)}, bf16[1,1024,768]{2,1,0:T(8,128)(2,1)}, u32[]{:S(2)}) copy-start(bf16[1,1024,768]{2,1,0:T(8,128)(2,1)} %param.55) | copy-start | bytes 4718596
  7.2 67.4 %all-gather.5.cloned.1.call-start = ((), (), s32[]{:S(2)}) async-start(), calls=%async_computation.4 | async-start | bytes 3649536 | tf_op jit(solution)/shard_map/all_gather | solution.py:261
  7.9 142.7 %all-gather.7.cloned.1.call-start = ((), (), s32[]{:S(2)}) async-start(), calls=%async_computation.5 | async-start | bytes 1216512 | tf_op jit(solution)/shard_map/all_gather | solution.py:263
  8.7 187.6 %all-gather.9.cloned.1.call-start = ((), (), s32[]{:S(2)}) async-start(), calls=%async_computation.6 | async-start | bytes 4866048 | tf_op jit(solution)/shard_map/all_gather | solution.py:271
  9.4 252.3 %all-gather.11.cloned.1.call-start = ((), (), s32[]{:S(2)}) async-start(), calls=%async_computation.7 | async-start | bytes 4866048 | tf_op jit(solution)/shard_map/all_gather | solution.py:273
  10.0 641.0 %reduce-scatter.7.cloned.1.call-start = ((), (), s32[]{:S(2)}) async-start(), calls=%async_computation.9 | async-start | bytes 2433024 | tf_op jit(solution)/shard_map/reduce_scatter | solution.py:323
  13.3 87.6 %copy-start.95 = (f32[512]{0:T(512)}, f32[512]{0:T(512)S(1)}, u32[]{:S(2)}) copy-start(f32[512]{0:T(512)S(1)} %broadcast_multiply_fusion.3) | copy-start | bytes 6148
  14.8 86.1 %copy-start.117 = (f32[512]{0:T(512)}, f32[512]{0:T(512)S(1)}, u32[]{:S(2)}) copy-start(f32[512]{0:T(512)S(1)} %fusion.228) | copy-start | bytes 6148
  14.8 52.1 %copy-start.131 = (s32[1024]{0:T(1024)}, s32[1024]{0:T(1024)S(1)}, u32[]{:S(2)}) copy-start(s32[1024]{0:T(1024)S(1)} %iota.49) | copy-start | bytes 12292
  64.5 36.4 %copy-start.78 = (f32[768]{0:T(1024)}, f32[768]{0:T(1024)S(1)}, u32[]{:S(2)}) copy-start(f32[768]{0:T(1024)S(1)} %convert_element_type.269) | copy-start | bytes 9220
  64.5 275.7 %copy-start.66 = (f32[768]{0:T(1024)}, f32[768]{0:T(1024)S(1)}, u32[]{:S(2)}) copy-start(f32[768]{0:T(1024)S(1)} %convert_element_type.278) | copy-start | bytes 9220
  64.5 36.3 %copy-start.91 = (f32[768]{0:T(1024)}, f32[768]{0:T(1024)S(1)}, u32[]{:S(2)}) copy-start(f32[768]{0:T(1024)S(1)} %convert_element_type.270) | copy-start | bytes 9220
  64.6 232.0 %copy-start.72 = (f32[768]{0:T(1024)}, f32[768]{0:T(1024)S(1)}, u32[]{:S(2)}) copy-start(f32[768]{0:T(1024)S(1)} %convert_element_type.279) | copy-start | bytes 9220
  66.2 88.0 %copy-start.4 = (bf16[1,1024,768]{1,2,0:T(8,128)(2,1)}, bf16[1,1024,768]{1,2,0:T(8,128)(2,1)S(1)}, u32[]{:S(2)}) copy-start(bf16[1,1024,768]{1,2,0:T(8,128)(2,1)S(1)} %copy.98) | copy-start | bytes 4718596
  66.5 15.8 %copy-start.93 = (f32[1024]{0:T(1024)}, f32[1024]{0:T(1024)S(1)}, u32[]{:S(2)}) copy-start(f32[1024]{0:T(1024)S(1)} %broadcast_multiply_fusion.1) | copy-start | bytes 12292
  67.0 15.4 %copy-start.123 = (f32[1024]{0:T(1024)}, f32[1024]{0:T(1024)S(1)}, u32[]{:S(2)}) copy-start(f32[1024]{0:T(1024)S(1)} %fusion.47) | copy-start | bytes 12292
  68.2 14.1 %copy-start.121 = (f32[1024]{0:T(1024)}, f32[1024]{0:T(1024)S(1)}, u32[]{:S(2)}) copy-start(f32[1024]{0:T(1024)S(1)} %fusion.226) | copy-start | bytes 12292
  97.0 20.3 %copy-start.97 = (f32[6,512]{1,0:T(8,128)}, f32[6,512]{1,0:T(8,128)S(1)}, u32[]{:S(2)}) copy-start(f32[6,512]{1,0:T(8,128)S(1)} %get-tuple-element.500) | copy-start | bytes 36868
  100.9 21.3 %copy-start.99 = (f32[6,512]{1,0:T(8,128)}, f32[6,512]{1,0:T(8,128)S(1)}, u32[]{:S(2)}) copy-start(f32[6,512]{1,0:T(8,128)S(1)} %get-tuple-element.502) | copy-start | bytes 36868
  153.0 122.3 %copy-start.119 = (f32[512]{0:T(512)}, f32[512]{0:T(512)S(1)}, u32[]{:S(2)}) copy-start(f32[512]{0:T(512)S(1)} %broadcast_multiply_fusion.2) | copy-start | bytes 6148
  153.3 122.0 %copy-start.127 = (f32[512]{0:T(512)}, f32[512]{0:T(512)S(1)}, u32[]{:S(2)}) copy-start(f32[512]{0:T(512)S(1)} %fusion.229) | copy-start | bytes 6148
  156.1 40.2 %copy-start.17 = (f32[512,768]{1,0:T(8,128)S(1)}, f32[512,768]{1,0:T(8,128)}, u32[]{:S(2)}) copy-start(f32[512,768]{1,0:T(8,128)} %copy-done.16) | copy-start | bytes 4718596
  156.1 184.1 %copy-start.74 = (f32[1024]{0:T(1024)}, f32[1024]{0:T(1024)S(1)}, u32[]{:S(2)}) copy-start(f32[1024]{0:T(1024)S(1)} %broadcast_multiply_fusion) | copy-start | bytes 12292
  158.1 182.2 %copy-start.76 = (f32[1024]{0:T(1024)}, f32[1024]{0:T(1024)S(1)}, u32[]{:S(2)}) copy-start(f32[1024]{0:T(1024)S(1)} %fusion.227) | copy-start | bytes 12292
  158.9 102.8 %copy-start.55 = (bf16[1,512,768]{2,1,0:T(8,128)(2,1)S(1)}, bf16[1,512,768]{2,1,0:T(8,128)(2,1)}, u32[]{:S(2)}) copy-start(bf16[1,512,768]{2,1,0:T(8,128)(2,1)} %param.70) | copy-start | bytes 2359300
  158.9 102.8 %copy-start.139 = (f32[3072]{0:T(1024)S(1)}, f32[3072]{0:T(1024)}, u32[]{:S(2)}) copy-start(f32[3072]{0:T(1024)} %convert_element_type.281) | copy-start | bytes 36868
  305.0 17.5 %copy-start.24 = (f32[1024,3072]{1,0:T(8,128)}, f32[1024,3072]{1,0:T(8,128)S(1)}, u32[]{:S(2)}) copy-start(f32[1024,3072]{1,0:T(8,128)S(1)} %fusion.239) | copy-start | bytes 37748740
  393.0 258.0 %reduce-scatter.5.cloned.1.call-start = ((), (), s32[]{:S(2)}) async-start(), calls=%async_computation.8 | async-start | bytes 7299072 | tf_op jit(solution)/shard_map/reduce_scatter | solution.py:321
  417.8 14.9 %slice-start = ((s8[12582912]{0:T(1024)(128)(4,1)}), s8[4194304]{0:T(1024)(128)(4,1)S(1)}, s32[]{:S(2)}) async-start(s8[12582912]{0:T(1024)(128)(4,1)} %bitcast.303), calls=%async_computation.12 | async-start | bytes 8388608
  505.8 259.5 %reduce-scatter.11.cloned.1.call-start = ((), (), s32[]{:S(2)}) async-start(), calls=%async_computation.11 | async-start | bytes 9732096 | tf_op jit(solution)/shard_map/reduce_scatter | solution.py:300
  529.7 377.8 %reduce-scatter.9.cloned.1.call-start = ((), (), s32[]{:S(2)}) async-start(), calls=%async_computation.10 | async-start | bytes 9732096 | tf_op jit(solution)/shard_map/reduce_scatter | solution.py:298
  580.1 46.8 %copy-start.126 = (f32[1024]{0:T(1024)S(1)}, f32[1024]{0:T(1024)}, u32[]{:S(2)}) copy-start(f32[1024]{0:T(1024)} %copy-done.125) | copy-start | bytes 12292
  (153 other events, 663.1 us)
Sparse Core Ops, SparseCore 0:
  11.0 63.4 all-gather.4
  77.6 52.9 all-gather.6
  133.6 62.6 all-gather.8
  199.2 62.4 all-gather.10
  393.1 97.9 reduce-scatter.6
  505.9 118.0 reduce-scatter.4
  630.5 134.7 reduce-scatter.10
  772.8 134.6 reduce-scatter.8
where the time goes:
time: 919 us; the launch traced here: 915 us
  waiting for transfers between devices  358 us (39%)
  matrix products  281 us (31%)
  local copies, waits for them, and re-layouts  99.4 us (11%)
  blocking collectives  84.1 us (9%)
  other arithmetic  73.7 us (8%)
  between operations  17.8 us (2%)
    reduce_scatter x1, waiting for transfers between devices, per_device(): lax.psum_scatter(mlp_totals[2], ('dp', 'fsdp'), scatter_dimension=0, tile...  142 us
    reduce_scatter x1, waiting for transfers between devices, per_device(): lax.psum_scatter(mlp_totals[4], ('dp', 'fsdp'), scatter_dimension=0, tile...  114 us
    unnamed x2, blocking collectives  84.1 us
    dot_general x8, matrix products, matmul_nt(): lax.dot_general(left, right, (((1,), (1,)), ((), ())), preferred_element_...  58.8 us
    all_gather x1, waiting for transfers between devices, per_device(): lax.all_gather(out_weight, ('dp', 'fsdp'), axis=0, tiled=True)  58.3 us
    dot_general x8, matrix products, matmul_tn(): lax.dot_general(left, right, (((0,), (0,)), ((), ())), preferred_element_...  52.7 us
    dot_general x8, matrix products, matmul(): return jnp.dot(left, right, preferred_element_type=jnp.float32)  52.1 us
    unnamed x383, local copies, waits for them, and re-layouts  48.1 us
  transfers between devices with their start and end apart: 8, of which 5 were waited for; matrix products, arithmetic and copies ran while one was open for 33% of the time, Pallas kernels for 0%

commit v1 on v0

v1 whole, which is shorter than its diff:
```python
import functools

import jax
import jax.numpy as jnp
from jax import lax
from jax.experimental import pallas as pl
from jax.experimental.pallas import tpu as pltpu
from jax.sharding import PartitionSpec as P

F32 = jnp.float32
BF16 = jnp.bfloat16
D = 768
FF = 3072
HEAD_DIM = 64
PAIRS = D // 128
TILE = 256
BRANCH = 0.14433756729740643
EPS = 1e-05
NEG = -1e30
VMEM_LIMIT = 60 * 2**20

LN1G, LN1B, QB, VB, PROJB, LN2G, LN2B, OUTB, FCB = 0, 1, 2, 3, 4, 5, 6, 7, 8


def dot(a, b):
    return jnp.dot(a, b, preferred_element_type=F32)


def dot_nt(a, b):
    return lax.dot_general(a, b, (((1,), (1,)), ((), ())), preferred_element_type=F32)


def dot_tn(a, b):
    return lax.dot_general(a, b, (((0,), (0,)), ((), ())), preferred_element_type=F32)


def normalize(x):
    center = x - jnp.mean(x, axis=-1, keepdims=True)
    rstd = lax.rsqrt(jnp.mean(center * center, axis=-1, keepdims=True) + EPS)
    return center * rstd, rstd


def norm_backward(g, n, rstd, gain):
    e = g * gain
    return rstd * (
        e
        - jnp.mean(e, axis=-1, keepdims=True)
        - n * jnp.mean(e * n, axis=-1, keepdims=True)
    )


def rows_of(base, tile):
    return pl.ds(pl.multiple_of(base + tile * TILE, TILE), TILE)


def lanes_of(start):
    return pl.ds(pl.multiple_of(start, 128), 128)


def group_refs(short, long):
    return ((short, 0), (long, short.shape[0]))


def qkv_tile(x_ref, table_ref, w_ref, a1_ref, qkv_ref, base, t):
    n, _ = normalize(x_ref[rows_of(0, t), :].astype(F32))
    a1 = (n * table_ref[LN1G : LN1G + 1, :] + table_ref[LN1B : LN1B + 1, :]).astype(BF16)
    rows = rows_of(base, t)
    a1_ref[rows, :] = a1
    for part, bias in ((0, QB), (1, None), (2, VB)):
        cols = slice(part * D, (part + 1) * D)
        out = dot(a1, w_ref[:, cols])
        if bias is not None:
            out = out + table_ref[bias : bias + 1, :]
        qkv_ref[rows, cols] = out.astype(BF16)


def attend_pair(split, qkv_ref, att_ref, lse_ref, base, length, pair):
    first = lax.broadcasted_iota(jnp.int32, (TILE, 128), 1) < HEAD_DIM
    head_lane = lax.broadcasted_iota(jnp.int32, (TILE, 128), 1)
    for qb in range(length // TILE):
        qrows = slice(base + qb * TILE, base + (qb + 1) * TILE)
        keys = (qb + 1) * TILE
        krows = slice(base, base + keys)
        q_pair = qkv_ref[qrows, lanes_of(pair * 128)] * BF16(HEAD_DIM**-0.5)
        k_pair = qkv_ref[krows, lanes_of(D + pair * 128)]
        v_pair = qkv_ref[krows, lanes_of(2 * D + pair * 128)]
        q_pos = qb * TILE + lax.broadcasted_iota(jnp.int32, (TILE, 1), 0)
        low = jnp.where(q_pos >= split, split, 0)
        k_pos = lax.broadcasted_iota(jnp.int32, (TILE, keys), 1)
        visible = (k_pos >= low) & (k_pos <= q_pos)
        outs = []
        lse_new = lse_ref[qrows, :]
        for half in (0, 1):
            mine = first if half == 0 else ~first
            s = dot_nt(jnp.where(mine, q_pair, BF16(0)), k_pair)
            s = jnp.where(visible, s, NEG)
            peak = jnp.max(s, axis=-1, keepdims=True)
            e = jnp.exp(s - peak)
            total = jnp.sum(e, axis=-1, keepdims=True)
            p = (e * (1.0 / total)).astype(BF16)
            outs.append(dot(p, v_pair))
            lse_new = jnp.where(head_lane == 2 * pair + half, peak + jnp.log(total), lse_new)
        lse_ref[qrows, :] = lse_new
        att_ref[qrows, lanes_of(pair * 128)] = jnp.where(first, outs[0], outs[1]).astype(BF16)


def mid_tile(x_ref, table_ref, w_ref, att_ref, mid_ref, base, t):
    rows = rows_of(base, t)
    out = dot(att_ref[rows, :], w_ref[:, 3 * D : 4 * D]) + table_ref[PROJB : PROJB + 1, :]
    mid_ref[rows, :] = x_ref[rows_of(0, t), :].astype(F32) + BRANCH * out


def forward_kernel(
    ssplit, lsplit, xs, xl, table_ref, w_ref, a1_ref, qkv_ref, att_ref, lse_t_ref, mid_ref, lse_ref
):
    for x_ref, base in group_refs(xs, xl):
        lax.fori_loop(
            0,
            x_ref.shape[0] // TILE,
            lambda t, c: (qkv_tile(x_ref, table_ref, w_ref, a1_ref, qkv_ref, base, t), c)[1],
            0,
        )
    lse_ref[...] = jnp.zeros_like(lse_ref)

    def pair_step(pair, c):
        attend_pair(ssplit[0], qkv_ref, att_ref, lse_ref, 0, xs.shape[0], pair)
        attend_pair(lsplit[0], qkv_ref, att_ref, lse_ref, xs.shape[0], xl.shape[0], pair)
        return c

    lax.fori_loop(0, PAIRS, pair_step, 0)
    lse_t_ref[...] = jnp.transpose(lse_ref[...])[:16, :]
    for x_ref, base in group_refs(xs, xl):
        lax.fori_loop(
            0,
            x_ref.shape[0] // TILE,
            lambda t, c: (mid_tile(x_ref, table_ref, w_ref, att_ref, mid_ref, base, t), c)[1],
            0,
        )


VM = pl.BlockSpec(memory_space=pltpu.VMEM)
SM = pl.BlockSpec(memory_space=pltpu.SMEM)


def forward_local(ssplit, lsplit, xs, xl, table, w_attn):
    rows = xs.shape[0] + xl.shape[0]
    return pl.pallas_call(
        forward_kernel,
        out_shape=(
            jax.ShapeDtypeStruct((rows, D), BF16),
            jax.ShapeDtypeStruct((rows, 3 * D), BF16),
            jax.ShapeDtypeStruct((rows, D), BF16),
            jax.ShapeDtypeStruct((16, rows), F32),
            jax.ShapeDtypeStruct((rows, D), F32),
        ),
        in_specs=[SM, SM, VM, VM, VM, VM],
        out_specs=[VM] * 5,
        scratch_shapes=[pltpu.VMEM((rows, 128), F32)],
        compiler_params=pltpu.CompilerParams(vmem_limit_bytes=VMEM_LIMIT),
        name="attention_forward",
    )(ssplit, lsplit, xs, xl, table, w_attn)


GELU_A = 0.7978845608028654
GELU_B = 0.044715


def mlp_tile(mid, g_out, table_ref, wf_ref, wo_ref):
    n2, rstd = normalize(mid)
    gain = table_ref[LN2G : LN2G + 1, :]
    a2 = (n2 * gain + table_ref[LN2B : LN2B + 1, :]).astype(BF16)
    g_mlp = (BRANCH * g_out).astype(BF16)
    out = None
    g_a2 = None
    acts, g_pres = [], []
    for j in range(FF // D):
        cols = slice(j * D, (j + 1) * D)
        pre = dot(a2, wf_ref[:, cols]) + table_ref[FCB + j : FCB + j + 1, :]
        g_act = dot_nt(g_mlp, wo_ref[cols, :])
        square = pre * pre
        t = jnp.tanh(pre * (GELU_A + (GELU_A * GELU_B) * square))
        half = 0.5 + 0.5 * t
        act = (pre * half).astype(BF16)
        slope = half + pre * (0.5 - 0.5 * t * t) * (GELU_A + (3 * GELU_A * GELU_B) * square)
        g_pre = (g_act * slope).astype(BF16)
        acts.append(act)
        g_pres.append(g_pre)
        part = dot(act, wo_ref[cols, :])
        out = part if out is None else out + part
        part = dot_nt(g_pre, wf_ref[:, cols])
        g_a2 = part if g_a2 is None else g_a2 + part
    out = mid + BRANCH * (out + table_ref[OUTB : OUTB + 1, :])
    g_mid = g_out + norm_backward(g_a2, n2, rstd, gain)
    return out, g_mid, a2, g_mlp, acts, g_pres, g_a2, n2


def colsum(x):
    return jnp.sum(x, axis=0, keepdims=True)


def mlp_kernel(
    n_tiles,
    slabs,
    mid_ref,
    cs_ref,
    cl_ref,
    table_ref,
    wf_ref,
    wo_ref,
    os_ref,
    ol_ref,
    g_mid_ref,
    sums_ref,
    dwf_ref,
    dwo_ref,
    a2_ref,
    g_mlp_ref,
    act_ref,
    g_pre_ref,
):
    step = pl.program_id(0)
    short_tiles = n_tiles[0]
    tiles = n_tiles[0] + n_tiles[1]

    @pl.when(step == 0)
    def _():
        sums_ref[...] = jnp.zeros_like(sums_ref)

    @pl.when(step < tiles)
    def _():
        cot = jnp.where(step < short_tiles, cs_ref[...], cl_ref[...]).astype(F32)
        out, g_mid, a2, g_mlp, acts, g_pres, g_a2, n2 = mlp_tile(
            mid_ref[...], cot, table_ref, wf_ref, wo_ref
        )
        out = out.astype(BF16)

        @pl.when(step < short_tiles)
        def _():
            os_ref[...] = out

        @pl.when(step >= short_tiles)
        def _():
            ol_ref[...] = out

        g_mid_ref[...] = g_mid
        rows = rows_of(0, step)
        a2_ref[rows, :] = a2
        g_mlp_ref[rows, :] = g_mlp
        sums_ref[0:1, :] += colsum(g_a2 * n2)
        sums_ref[1:2, :] += colsum(g_a2)
        sums_ref[2:3, :] += colsum(g_mlp.astype(F32))
        for j in range(FF // D):
            act_ref[rows, j * D : (j + 1) * D] = acts[j]
            g_pre_ref[rows, j * D : (j + 1) * D] = g_pres[j]
            sums_ref[3 + j : 4 + j, :] += colsum(g_pres[j].astype(F32))

    for j in range(4):

        @pl.when(step == tiles + j)
        def _(j=j):
            res = dot_tn(act_ref[:, j * D : (j + 1) * D], g_mlp_ref[...])
            if slabs:
                dwo_ref[...] = res.astype(BF16).reshape(dwo_ref.shape)
            else:
                dwo_ref[...] = res

    for j in range(2 if slabs else 4):

        @pl.when(step == tiles + 4 + j)
        def _(j=j):
            if slabs:
                dev = D // 24
                left = dot_tn(a2_ref[...], g_pre_ref[:, 2 * j * D : (2 * j + 1) * D])
                right = dot_tn(a2_ref[...], g_pre_ref[:, (2 * j + 1) * D : (2 * j + 2) * D])
                both = jnp.concatenate(
                    [left.reshape(dev, 24, D), right.reshape(dev, 24, D)], axis=1
                )
                dwf_ref[...] = both.astype(BF16)
            else:
                dwf_ref[...] = dot_tn(a2_ref[...], g_pre_ref[:, j * D : (j + 1) * D])


def mlp_local(mid, cs, cl, table, w_fc, w_out, slabs):
    rows = mid.shape[0]
    ns, nl = cs.shape[0] // TILE, cl.shape[0] // TILE
    tiles = ns + nl
    steps = tiles + (6 if slabs else 8)
    whole = lambda shape: pl.BlockSpec(shape, lambda i: (0, 0), pipeline_mode=pl.Buffered(1))
    tile = lambda f: pl.BlockSpec((TILE, D), f)
    short_at = lambda i: (jnp.minimum(i, ns - 1), 0)
    long_at = lambda i: (jnp.clip(i - ns, 0, nl - 1), 0)
    all_at = lambda i: (jnp.minimum(i, tiles - 1), 0)
    if slabs:
        dev = D // 24
        dwo_shape = jax.ShapeDtypeStruct((dev, 96, D), BF16)
        dwo_spec = pl.BlockSpec((dev // 4, 96, D), lambda i: (jnp.clip(i - tiles, 0, 3), 0, 0))
        dwf_shape = jax.ShapeDtypeStruct((dev, 96, D), BF16)
        dwf_spec = pl.BlockSpec((dev, 48, D), lambda i: (0, jnp.clip(i - tiles - 4, 0, 1), 0))
    else:
        dwo_shape = jax.ShapeDtypeStruct((FF, D), F32)
        dwo_spec = pl.BlockSpec((D, D), lambda i: (jnp.clip(i - tiles, 0, 3), 0))
        dwf_shape = jax.ShapeDtypeStruct((D, FF), F32)
        dwf_spec = pl.BlockSpec((D, D), lambda i: (0, jnp.clip(i - tiles - 4, 0, 3)))
    return pl.pallas_call(
        functools.partial(mlp_kernel, (ns, nl), slabs),
        grid=(steps,),
        out_shape=(
            jax.ShapeDtypeStruct(cs.shape, BF16),
            jax.ShapeDtypeStruct(cl.shape, BF16),
            jax.ShapeDtypeStruct((rows, D), F32),
            jax.ShapeDtypeStruct((8, D), F32),
            dwf_shape,
            dwo_shape,
        ),
        in_specs=[
            tile(all_at),
            tile(short_at),
            tile(long_at),
            whole(table.shape),
            whole(w_fc.shape),
            whole(w_out.shape),
        ],
        out_specs=[
            tile(short_at),
            tile(long_at),
            tile(all_at),
            pl.BlockSpec((8, D), lambda i: (0, 0)),
            dwf_spec,
            dwo_spec,
        ],
        scratch_shapes=[
            pltpu.VMEM((rows, D), BF16),
            pltpu.VMEM((rows, D), BF16),
            pltpu.VMEM((rows, FF), BF16),
            pltpu.VMEM((rows, FF), BF16),
        ],
        compiler_params=pltpu.CompilerParams(vmem_limit_bytes=VMEM_LIMIT),
        name="mlp",
    )(mid, cs, cl, table, w_fc, w_out)


def proj_back_tile(g_mid_ref, w_ref, g_attn_ref, g_att_ref, sums_ref, t):
    rows = rows_of(0, t)
    g_attn = (BRANCH * g_mid_ref[rows, :]).astype(BF16)
    g_attn_ref[rows, :] = g_attn
    g_att_ref[rows, :] = dot_nt(g_attn, w_ref[:, 3 * D : 4 * D]).astype(BF16)
    sums_ref[PROJB : PROJB + 1, :] += colsum(g_attn.astype(F32))


def attend_back_pair(split, qkv_ref, g_att_ref, lse_t_ref, g_qkv_ref, dk_ref, dv_ref, base, length, pair):
    first = lax.broadcasted_iota(jnp.int32, (TILE, 128), 1) < HEAD_DIM
    dk_ref[0:length, :] = jnp.zeros((length, 128), F32)
    dv_ref[0:length, :] = jnp.zeros((length, 128), F32)
    for qb in range(length // TILE):
        qrows = slice(base + qb * TILE, base + (qb + 1) * TILE)
        keys = (qb + 1) * TILE
        krows = slice(base, base + keys)
        q_pair = qkv_ref[qrows, lanes_of(pair * 128)] * BF16(HEAD_DIM**-0.5)
        g_pair = g_att_ref[qrows, lanes_of(pair * 128)]
        k_pair = qkv_ref[krows, lanes_of(D + pair * 128)]
        v_pair = qkv_ref[krows, lanes_of(2 * D + pair * 128)]
        q_pos = qb * TILE + lax.broadcasted_iota(jnp.int32, (1, TILE), 1)
        low = jnp.where(q_pos >= split, split, 0)
        k_pos = lax.broadcasted_iota(jnp.int32, (keys, TILE), 0)
        visible = (k_pos >= low) & (k_pos <= q_pos)
        dqs = []
        dk = dk_ref[0:keys, :]
        dv = dv_ref[0:keys, :]
        for half in (0, 1):
            mine = first if half == 0 else ~first
            q_half = jnp.where(mine, q_pair, BF16(0))
            g_half = jnp.where(mine, g_pair, BF16(0))
            lse = lse_t_ref[pl.ds(2 * pair + half, 1), qrows]
            s = jnp.where(visible, dot_nt(k_pair, q_half), NEG)
            p = jnp.exp(s - lse)
            dp = dot_nt(v_pair, g_half)
            inner = jnp.sum(p * dp, axis=0, keepdims=True)
            ds = (p * (dp - inner)).astype(BF16)
            dv = dv + dot(p.astype(BF16), g_half)
            dk = dk + dot(ds, q_half)
            dqs.append(dot_tn(ds, k_pair))
        dk_ref[0:keys, :] = dk
        dv_ref[0:keys, :] = dv
        dq = jnp.where(first, dqs[0], dqs[1]) * (HEAD_DIM**-0.5)
        g_qkv_ref[qrows, lanes_of(pair * 128)] = dq.astype(BF16)
    all_rows = slice(base, base + length)
    g_qkv_ref[all_rows, lanes_of(D + pair * 128)] = dk_ref[0:length, :].astype(BF16)
    g_qkv_ref[all_rows, lanes_of(2 * D + pair * 128)] = dv_ref[0:length, :].astype(BF16)


def ln1_back_tile(x_ref, g_mid_ref, table_ref, w_ref, g_qkv_ref, gx_ref, sums_ref, base, t):
    rows = rows_of(base, t)
    g_qkv = g_qkv_ref[rows, :]
    g_a1 = dot_nt(g_qkv, w_ref[:, 0 : 3 * D])
    own = rows_of(0, t)
    n, rstd = normalize(x_ref[own, :].astype(F32))
    gx_ref[own, :] = g_mid_ref[rows, :] + norm_backward(
        g_a1, n, rstd, table_ref[LN1G : LN1G + 1, :]
    )
    sums_ref[LN1G : LN1G + 1, :] += colsum(g_a1 * n)
    sums_ref[LN1B : LN1B + 1, :] += colsum(g_a1)
    sums_ref[QB : QB + 1, :] += colsum(g_qkv[:, 0:D].astype(F32))
    sums_ref[VB : VB + 1, :] += colsum(g_qkv[:, 2 * D : 3 * D].astype(F32))


def backward_kernel(
    ssplit,
    lsplit,
    xs,
    xl,
    table_ref,
    w_ref,
    a1_ref,
    qkv_ref,
    att_ref,
    lse_t_ref,
    g_mid_ref,
    gxs_ref,
    gxl_ref,
    dwp_ref,
    dwq_ref,
    sums_ref,
    g_attn_ref,
    g_att_ref,
    g_qkv_ref,
    dk_ref,
    dv_ref,
):
    sums_ref[...] = jnp.zeros_like(sums_ref)
    rows = xs.shape[0] + xl.shape[0]
    lax.fori_loop(
        0,
        rows // TILE,
        lambda t, c: (
            proj_back_tile(g_mid_ref, w_ref, g_attn_ref, g_att_ref, sums_ref, t),
            c,
        )[1],
        0,
    )
    dwp_ref[...] = dot_tn(att_ref[...], g_attn_ref[...])

    def pair_step(pair, c):
        for split, x_ref, base in ((ssplit[0], xs, 0), (lsplit[0], xl, xs.shape[0])):
            attend_back_pair(
                split, qkv_ref, g_att_ref, lse_t_ref, g_qkv_ref, dk_ref, dv_ref, base, x_ref.shape[0], pair
            )
        return c

    lax.fori_loop(0, PAIRS, pair_step, 0)
    for j in range(3):
        dwq_ref[:, j * D : (j + 1) * D] = dot_tn(a1_ref[...], g_qkv_ref[:, j * D : (j + 1) * D])
    for x_ref, gx_ref, base in ((xs, gxs_ref, 0), (xl, gxl_ref, xs.shape[0])):
        lax.fori_loop(
            0,
            x_ref.shape[0] // TILE,
            lambda t, c: (
                ln1_back_tile(
                    x_ref, g_mid_ref, table_ref, w_ref, g_qkv_ref, gx_ref, sums_ref, base, t
                ),
                c,
            )[1],
            0,
        )


def backward_local(ssplit, lsplit, xs, xl, table, w_attn, a1, qkv, att, lse_t, g_mid):
    rows = xs.shape[0] + xl.shape[0]
    return pl.pallas_call(
        backward_kernel,
        out_shape=(
            jax.ShapeDtypeStruct(xs.shape, F32),
            jax.ShapeDtypeStruct(xl.shape, F32),
            jax.ShapeDtypeStruct((D, D), F32),
            jax.ShapeDtypeStruct((D, 3 * D), F32),
            jax.ShapeDtypeStruct((8, D), F32),
        ),
        in_specs=[SM, SM] + [VM] * 9,
        out_specs=[VM] * 5,
        scratch_shapes=[
            pltpu.VMEM((rows, D), BF16),
            pltpu.VMEM((rows, D), BF16),
            pltpu.VMEM((rows, 3 * D), BF16),
            pltpu.VMEM((xl.shape[0], 128), F32),
            pltpu.VMEM((xl.shape[0], 128), F32),
        ],
        compiler_params=pltpu.CompilerParams(vmem_limit_bytes=VMEM_LIMIT),
        name="attention_backward",
    )(ssplit, lsplit, xs, xl, table, w_attn, a1, qkv, att, lse_t, g_mid)


AXES = ("dp", "fsdp")


def gather(x, axis=0):
    return lax.all_gather(x, AXES, axis=axis, tiled=True)


def scatter(x):
    return lax.psum_scatter(x, AXES, scatter_dimension=0, tiled=True)


def general(args, devices):
    (st, lt, ss, ls, ln1g, ln1b, wqkv, qvb, wproj, projb, ln2g, ln2b, wfc, fcb, wout, outb, sc, lc) = args
    xs, xl = st.reshape(-1, D), lt.reshape(-1, D)
    cs, cl = sc.reshape(-1, D), lc.reshape(-1, D)
    vectors = (ln1g, ln1b, qvb, projb, ln2g, ln2b, outb, fcb)
    sizes = [v.shape[0] for v in vectors]
    every = lax.all_gather(jnp.concatenate(vectors), AXES, axis=0)
    starts = [sum(sizes[:i]) for i in range(len(sizes))]
    full = [every[:, s : s + n].reshape(-1, D) for s, n in zip(starts, sizes)]
    table = jnp.concatenate(full + [jnp.zeros((4, D), BF16)]).astype(F32)
    w_attn = gather(jnp.concatenate([wqkv, wproj], axis=1))
    w_fc, w_out = gather(wfc), gather(wout)
    a1, qkv, att, lse_t, mid = forward_local(ss, ls, xs, xl, table, w_attn)
    out_s, out_l, g_mid, sums2, dwf, dwo = mlp_local(mid, cs, cl, table, w_fc, w_out, False)
    gxs, gxl, dwp, dwq, sums1 = backward_local(
        ss, ls, xs, xl, table, w_attn, a1, qkv, att, lse_t, g_mid
    )
    rs = lambda x: x.reshape(devices, -1)
    small = jnp.concatenate(
        [
            rs(sums1[0]),
            rs(sums1[1]),
            rs(sums1[2:4]),
            rs(sums1[4]),
            rs(sums2[0]),
            rs(sums2[1]),
            rs(sums2[2]),
            rs(sums2[3:7]),
        ],
        axis=1,
    )
    small = scatter(small)[0]
    parts = [small[s : s + n] for s, n in zip(starts, sizes)]
    d_ln1g, d_ln1b, d_qvb, d_projb, d_ln2g, d_ln2b, d_outb, d_fcb = parts
    return (
        out_s.reshape(st.shape),
        out_l.reshape(lt.shape),
        gxs.reshape(st.shape),
        gxl.reshape(lt.shape),
        d_ln1g,
        d_ln1b,
        scatter(dwq),
        d_qvb,
        scatter(dwp),
        d_projb,
        d_ln2g,
        d_ln2b,
        scatter(dwf),
        d_fcb,
        scatter(dwo),
        d_outb,
    )


def per_device(devices, *args):
    return general(args, devices)


def solution(mesh):
    vec, mat, seq = P(AXES), P(AXES, None), P(AXES, None, None)
    in_specs = (seq, seq, vec, vec) + (vec, vec, mat, vec, mat, vec) * 1 + (vec, vec, mat, vec, mat, vec) + (seq, seq)
    out_specs = (seq,) * 4 + (vec, vec, mat, vec, mat, vec) * 2
    return jax.shard_map(
        functools.partial(per_device, mesh.size),
        mesh=mesh,
        in_specs=in_specs,
        out_specs=out_specs,
        check_vma=False,
    )
```

time: 919 us -> 883 us (0.961)
  matrix products: 281 us -> 0 us
  Pallas kernels: 0 us -> 207 us
  waiting for transfers between devices: 358 us -> 558 us
  local copies, waits for them, and re-layouts: 99.4 us -> 9.46 us
  other arithmetic: 73.7 us -> 2.22 us
    dot_general x60 -> x0, matrix products: 281 us -> none  [the longest x8 58.8 us: matmul_nt(): lax.dot_general(left, right, (((1,), (1,)), ((), ())), preferred_element_...]
    pallas_call x0 -> x3, Pallas kernels: none -> 207 us  [the longest x1 80.5 us: mlp_local(): pl.pallas_call(functools.partial(mlp_kernel, (ns, nl), slabs), grid=(step...]
    reduce_scatter x4, waiting for transfers between devices: 256 us -> 462 us  [scatter(): return lax.psum_scatter(x, AXES, scatter_dimension=0, tiled=True)]
    unnamed x383 -> x6, local copies, waits for them, and re-layouts: 48.1 us -> 0.28 us
    convert_element_type x13 -> x1, other arithmetic: 30.3 us -> 0.63 us  [general(): table = jnp.concatenate(full + [jnp.zeros((4, D), BF16)]).astype(F32)]
    reduce_sum x22 -> x0, other arithmetic: 29 us -> none  [the longest x6 10.4 us: attend_forward(): totals = jnp.sum(exponent, axis=-1, keepdims=True)]
    scatter-add x6 -> x0, local copies, waits for them, and re-layouts: 21.6 us -> none  [the longest x2 8.3 us: attend_backward(): grad_value.at[:row_stop, head_start:head_stop]]
    convert_element_type x3 -> x0, local copies, waits for them, and re-layouts: 12.8 us -> none  [the longest x2 11.4 us: attention_group(): mixed = (matmul(norm_one, qkv_weights) + shift_full).astype(jnp.bfloat16)]
  transfers between devices with their start and end apart: 8 -> 7, of which waited for: 5 -> 7; matrix products, arithmetic and copies ran while one was open for 33% -> 1% of each run, Pallas kernels for 0% -> 6%
where the time goes in v1:
time: 883 us; the launch traced here: 876 us
  waiting for transfers between devices  558 us (63%)
  Pallas kernels  207 us (23%)
  blocking collectives  82.4 us (9%)
  between operations  15.8 us (2%)
  local copies, waits for them, and re-layouts  9.46 us (1%)
    reduce_scatter x4, waiting for transfers between devices, scatter(): return lax.psum_scatter(x, AXES, scatter_dimension=0, tiled=True)  462 us
    all_gather x3, waiting for transfers between devices, gather(): return lax.all_gather(x, AXES, axis=axis, tiled=True)  93.5 us
    unnamed x2, blocking collectives  82.4 us
    pallas_call x1, Pallas kernels, mlp_local(): pl.pallas_call(functools.partial(mlp_kernel, (ns, nl), slabs), grid=(step...  80.5 us
    pallas_call x1, Pallas kernels, backward_local(): pl.pallas_call(backward_kernel, out_shape=(jax.ShapeDtypeStruct(xs.shape,...  72.2 us
    pallas_call x1, Pallas kernels, forward_local(): pl.pallas_call(forward_kernel, out_shape=(jax.ShapeDtypeStruct((rows, D),...  54.2 us
  transfers between devices with their start and end apart: 7, of which 7 were waited for; matrix products, arithmetic and copies ran while one was open for 1% of the time, Pallas kernels for 6%

profile of v1, /device:TPU:0, one launch (start us, length us, event | category | flops | bytes accessed | tf_op | source)
XLA Modules:
  0.0 875.6 jit_solution(14787485305151870703)
XLA Ops:
  7.2 1.6 pad_maximum_fusion
  8.9 0.7 all-gather.7.cloned.1.call-update
  9.6 0.7 all-gather.9.cloned.1.call-update
  10.4 5.4 concatenate.12
  15.8 0.2 dynamic-update-slice
  16.1 42.4 %all-reduce = bf16[9216]{0:T(1024)(128)(2,1)S(1)} all-reduce(bf16[9216]{0:T(1024)(128)(2,1)S(1)} %dynamic-update-slice), channel_id=2, replica_groups=mesh['dp'=4,'fsdp'=8] {'dp','fsdp'}, use_global_device_ids=true, to_apply=%add | all-reduce | flops 9216 | bytes 36864
  58.5 0.1 reshape.112
  58.8 0.1 reshape.100
  58.9 0.1 reshape.101
  59.0 0.1 reshape.102
  59.1 0.1 reshape.96
  59.2 0.1 reshape.97
  59.3 0.1 reshape.99
  59.7 0.6 convert_element_type.3.table_ref
  61.6 16.7 %all-gather.5.cloned.1.call-done.w_ref = bf16[768,3072]{1,0:T(8,128)(2,1)} async-done(((bf16[24,3072]{1,0:T(8,128)(2,1)}), bf16[768,3072]{1,0:T(8,128)(2,1)}) %all-gather.5.cloned.1.call-update) | async-done | bytes 4718608 | tf_op jit(solution)/shard_map/all_gather | solution.py:495
  78.3 54.2 %attention_forward.1 = (bf16[1536,768]{1,0:T(8,128)(2,1)}, bf16[1536,2304]{1,0:T(8,128)(2,1)}, bf16[1536,768]{1,0:T(8,128)(2,1)}, f32[16,1536]{1,0:T(8,128)}, f32[1536,768]{1,0:T(8,128)}) custom-call(s32[1]{0:T(128)S(6)} %copy.35.ssplit, s32[1]{0:T(128)S(6)} %copy.36.lsplit, bf16[512,768]{1,0:T(8,128)(2,1)} %bitcast.26, bf16[1024,768]{1,0:T(8,128)(2,1)} %bitcast.24, ...), custom_call_target="tpu_custom_call" | custom-call | tf_op jit(solution)/shard_map/attention_forward/pallas_call | solution.py:147
  132.5 11.3 %all-gather.7.cloned.1.call-done.wf_ref = bf16[768,3072]{1,0:T(8,128)(2,1)} async-done(((bf16[24,3072]{1,0:T(8,128)(2,1)}), bf16[768,3072]{1,0:T(8,128)(2,1)}) %all-gather.7.cloned.1.call-update) | async-done | bytes 4718608 | tf_op jit(solution)/shard_map/all_gather | solution.py:495
  143.8 65.5 %all-gather.9.cloned.1.call-done.wo_ref = bf16[3072,768]{1,0:T(8,128)(2,1)} async-done(((bf16[96,768]{1,0:T(8,128)(2,1)}), bf16[3072,768]{1,0:T(8,128)(2,1)}) %all-gather.9.cloned.1.call-update) | async-done | bytes 4718608 | tf_op jit(solution)/shard_map/all_gather | solution.py:495
  209.3 80.5 %mlp.1 = (bf16[512,768]{1,0:T(8,128)(2,1)}, bf16[1024,768]{1,0:T(8,128)(2,1)}, f32[1536,768]{1,0:T(8,128)}, f32[8,768]{1,0:T(8,128)}, f32[768,3072]{1,0:T(8,128)}, /*index=5*/f32[3072,768]{1,0:T(8,128)}) custom-call(f32[1536,768]{1,0:T(8,128)} %get-tuple-element.32.mid_ref, bf16[512,768]{1,0:T(8,128)(2,1)} %bitcast.29, bf16[1024,768]{1,0:T(8,128)(2,1)} %bitcast.28, ...), custom_call_target="tpu_custom_call" | custom-call | tf_op jit(solution)/shard_map/mlp/pallas_call | solution.py:304
  289.9 72.2 %attention_backward.1 = (f32[512,768]{1,0:T(8,128)}, f32[1024,768]{1,0:T(8,128)}, f32[768,768]{1,0:T(8,128)}, f32[768,2304]{1,0:T(8,128)}, f32[8,768]{1,0:T(8,128)}) custom-call(s32[1]{0:T(128)S(6)} %copy.35.ssplit, s32[1]{0:T(128)S(6)} %copy.36.lsplit, bf16[512,768]{1,0:T(8,128)(2,1)} %bitcast.27, bf16[1024,768]{1,0:T(8,128)(2,1)} %bitcast.25, ...), custom_call_target="tpu_custom_call" | custom-call | tf_op jit(solution)/shard_map/attention_backward/pallas_call | solution.py:468
  362.1 0.5 reduce-scatter.5.cloned.1.call-update
  362.7 0.5 reduce-scatter.11.cloned.1.call-update
  363.3 0.7 reduce-scatter.9.cloned.1.call-update
  364.8 0.1 concatenate.15
  364.9 40.0 %all-reduce.1 = f32[32,288]{1,0:T(8,128)S(1)} all-reduce(f32[32,288]{1,0:T(8,128)S(1)} %concatenate.15), channel_id=3, replica_groups=mesh['dp'=4,'fsdp'=8] {'dp','fsdp'}, use_global_device_ids=true, to_apply=%region_0.0.clone | all-reduce | flops 9216 | bytes 73728
  404.9 0.6 dynamic-slice_bitcast_fusion.1
  405.5 0.6 dynamic-slice_bitcast_fusion.5
  406.1 0.6 dynamic-slice_bitcast_fusion
  406.7 53.4 %reduce-scatter.7.cloned.1.call-done = f32[24,768]{1,0:T(8,128)} async-done(((f32[768,768]{1,0:T(8,128)}), f32[24,768]{1,0:T(8,128)}) %reduce-scatter.7.cloned.1.call-update) | async-done | bytes 73744 | tf_op jit(solution)/shard_map/reduce_scatter | solution.py:499
  460.0 125.2 %reduce-scatter.5.cloned.1.call-done = f32[24,2304]{1,0:T(8,128)} async-done(((f32[768,2304]{1,0:T(8,128)}), f32[24,2304]{1,0:T(8,128)}) %reduce-scatter.5.cloned.1.call-update) | async-done | bytes 221200 | tf_op jit(solution)/shard_map/reduce_scatter | solution.py:499
  585.2 141.2 %reduce-scatter.11.cloned.1.call-done = f32[96,768]{1,0:T(8,128)} async-done(((f32[3072,768]{1,0:T(8,128)}), f32[96,768]{1,0:T(8,128)}) %reduce-scatter.11.cloned.1.call-update) | async-done | bytes 294928 | tf_op jit(solution)/shard_map/reduce_scatter | solution.py:499
  726.4 142.2 %reduce-scatter.9.cloned.1.call-done = f32[24,3072]{1,0:T(8,128)} async-done(((f32[768,3072]{1,0:T(8,128)}), f32[24,3072]{1,0:T(8,128)}) %reduce-scatter.9.cloned.1.call-update) | async-done | bytes 294928 | tf_op jit(solution)/shard_map/reduce_scatter | solution.py:499
  (33 shorter events, 1.5 us)
Async XLA Ops:
  7.2 71.1 %all-gather.5.cloned.1.call-start = ((), (), s32[]{:S(2)}) async-start(), calls=%async_computation.4 | async-start | bytes 4866048 | tf_op jit(solution)/shard_map/all_gather | solution.py:495
  8.8 135.0 %all-gather.7.cloned.1.call-start = ((), (), s32[]{:S(2)}) async-start(), calls=%async_computation.5 | async-start | bytes 4866048 | tf_op jit(solution)/shard_map/all_gather | solution.py:495
  9.6 199.7 %all-gather.9.cloned.1.call-start = ((), (), s32[]{:S(2)}) async-start(), calls=%async_computation.6 | async-start | bytes 4866048 | tf_op jit(solution)/shard_map/all_gather | solution.py:495
  10.3 449.7 %reduce-scatter.7.cloned.1.call-start = ((), (), s32[]{:S(2)}) async-start(), calls=%async_computation.8 | async-start | bytes 2433024 | tf_op jit(solution)/shard_map/reduce_scatter | solution.py:499
  362.0 223.2 %reduce-scatter.5.cloned.1.call-start = ((), (), s32[]{:S(2)}) async-start(), calls=%async_computation.7 | async-start | bytes 7299072 | tf_op jit(solution)/shard_map/reduce_scatter | solution.py:499
  362.6 363.8 %reduce-scatter.11.cloned.1.call-start = ((), (), s32[]{:S(2)}) async-start(), calls=%async_computation.10 | async-start | bytes 9732096 | tf_op jit(solution)/shard_map/reduce_scatter | solution.py:499
  363.2 505.4 %reduce-scatter.9.cloned.1.call-start = ((), (), s32[]{:S(2)}) async-start(), calls=%async_computation.9 | async-start | bytes 9732096 | tf_op jit(solution)/shard_map/reduce_scatter | solution.py:499
  363.3 0.7 copy-start.1
  363.3 1.1 copy-start
Sparse Core Ops, SparseCore 0:
  11.6 66.6 all-gather.4
  81.3 62.4 all-gather.6
  146.9 62.4 all-gather.8
  362.2 97.8 reduce-scatter.6
  467.1 118.1 reduce-scatter.4
  591.6 134.7 reduce-scatter.10
  733.9 134.6 reduce-scatter.8

commit v2 on v1

--- a/solution.py
+++ b/solution.py
@@ -57,15 +57,23 @@
     return pl.ds(pl.multiple_of(start, 128), 128)
 
 
+def loop(count, body):
+    lax.fori_loop(0, count, lambda i, c: (body(i), c)[1], 0)
+
+
 def group_refs(short, long):
     return ((short, 0), (long, short.shape[0]))
 
 
-def qkv_tile(x_ref, table_ref, w_ref, a1_ref, qkv_ref, base, t):
+def norm_tile(x_ref, table_ref, a1_ref, base, t):
     n, _ = normalize(x_ref[rows_of(0, t), :].astype(F32))
-    a1 = (n * table_ref[LN1G : LN1G + 1, :] + table_ref[LN1B : LN1B + 1, :]).astype(BF16)
-    rows = rows_of(base, t)
-    a1_ref[rows, :] = a1
+    a1 = n * table_ref[LN1G : LN1G + 1, :] + table_ref[LN1B : LN1B + 1, :]
+    a1_ref[rows_of(base, t), :] = a1.astype(BF16)
+
+
+def qkv_tile(table_ref, w_ref, a1_ref, qkv_ref, t):
+    rows = rows_of(0, t)
+    a1 = a1_ref[rows, :]
     for part, bias in ((0, QB), (1, None), (2, VB)):
         cols = slice(part * D, (part + 1) * D)
         out = dot(a1, w_ref[:, cols])
@@ -114,12 +122,8 @@
     ssplit, lsplit, xs, xl, table_ref, w_ref, a1_ref, qkv_ref, att_ref, lse_t_ref, mid_ref, lse_ref
 ):
     for x_ref, base in group_refs(xs, xl):
-        lax.fori_loop(
-            0,
-            x_ref.shape[0] // TILE,
-            lambda t, c: (qkv_tile(x_ref, table_ref, w_ref, a1_ref, qkv_ref, base, t), c)[1],
-            0,
-        )
+        loop(x_ref.shape[0] // TILE, lambda t: norm_tile(x_ref, table_ref, a1_ref, base, t))
+    loop(a1_ref.shape[0] // TILE, lambda t: qkv_tile(table_ref, w_ref, a1_ref, qkv_ref, t))
     lse_ref[...] = jnp.zeros_like(lse_ref)
 
     def pair_step(pair, c):
@@ -488,6 +492,438 @@
     )(ssplit, lsplit, xs, xl, table, w_attn, a1, qkv, att, lse_t, g_mid)
 
 
+MESH = pl.DeviceIdType.MESH
+COLS, DEPTH = 4, 4
+
+
+class Place:
+    def __init__(self):
+        q, f = lax.axis_index("dp"), lax.axis_index("fsdp")
+        z = lax.div(f, 2)
+        self.core = lax.rem(f, 2)
+        self.col = [q, q + 1 - 2 * lax.rem(q, 2), lax.rem(q + 2, 4), 3 - q]
+        self.depth = [lax.rem(z + k, DEPTH) for k in range(DEPTH)]
+        self.index = q * 2 * DEPTH + f
+        self.partner = (q, 2 * z + 1 - self.core)
+        self.x = (self.col[1], f)
+        self.y = (self.col[2], f)
+        self.along = [(q, 2 * d + self.core) for d in self.depth]
+
+    def greet(self):
+        barrier = pltpu.get_barrier_semaphore()
+        others = [self.partner, self.x, self.y] + self.along[1:]
+        for device in others:
+            pl.semaphore_signal(barrier, inc=1, device_id=device, device_id_type=MESH)
+        pl.semaphore_wait(barrier, len(others))
+
+
+def remote(src, dst, send, recv, device):
+    return pltpu.make_async_remote_copy(
+        src_ref=src, dst_ref=dst, send_sem=send, recv_sem=recv, device_id=device, device_id_type=MESH
+    )
+
+
+def at(start, size, step):
+    return pl.ds(pl.multiple_of(start, step), size)
+
+
+Z, X, Y, ACROSS, PAIR = 0, 3, 7, 11, 15
+N_GATHER = 31
+Y_PATH = (0, 3)
+
+
+class Gather:
+    def __init__(self, place, full, own, wide, send, recv):
+        self.place, self.full, self.own, self.wide = place, full, own, wide
+        self.send, self.recv = send, recv
+        self.spots = {}
+        for core in (0, 1):
+            c = place.core if core == 0 else 1 - place.core
+            for r in range(COLS):
+                for k in range(DEPTH):
+                    chip = place.col[r] * DEPTH + place.depth[k]
+                    if wide:
+                        half = full.shape[1] // 2
+                        spot = full.at[at(chip * 48, 48, 16), at(c * half, half, 128)]
+                    else:
+                        spot = full.at[at((chip * 2 + c) * 96, 96, 16), :]
+                    self.spots[core, r, k] = spot
+
+    def copy(self, kind, r, k, arriving=False):
+        place = self.place
+        here = self.spots[0, r, k]
+        src = self.own if (r, k) == (0, 0) and not arriving else here
+        if kind == Z:
+            n, device = (DEPTH - k if not arriving else k) - 1, place.along[k]
+            src, here = (self.own, self.spots[0, 0, 0]) if not arriving else (here, here)
+        elif kind == X:
+            n, device = X + k, place.x
+        elif kind == Y:
+            n, device = Y + k, place.y
+        elif kind == ACROSS:
+            n, device = ACROSS + k, (place.y if k in Y_PATH else place.x)
+        else:
+            n, device = PAIR + 4 * r + k, place.partner
+            if arriving:
+                src = here = self.spots[1, r, k]
+        sent = n if kind != Z else k - 1
+        return remote(src, here, self.send.at[sent], self.recv.at[n], device)
+
+    def begin(self):
+        for k in range(1, DEPTH):
+            self.copy(Z, 0, k).start()
+        self.spread(0)
+
+    def spread(self, k):
+        self.copy(X, 0, k).start()
+        self.copy(Y, 0, k).start()
+        self.copy(PAIR, 0, k).start()
+
+    def along(self, k):
+        self.copy(Z, 0, k, True).wait_recv()
+        self.spread(k)
+
+    def across(self, k):
+        self.copy(X, 1, k, True).wait_recv()
+        if k in Y_PATH:
+            self.copy(ACROSS, 1, k).start()
+        self.copy(PAIR, 1, k).start()
+        self.copy(Y, 2, k, True).wait_recv()
+        if k not in Y_PATH:
+            self.copy(ACROSS, 2, k).start()
+        self.copy(PAIR, 2, k).start()
+
+    def last(self, k):
+        self.copy(ACROSS, 3, k, True).wait_recv()
+        self.copy(PAIR, 3, k).start()
+
+    def arrive(self):
+        for r in range(COLS):
+            for k in range(DEPTH):
+                self.copy(PAIR, r, k, True).wait_recv()
+
+    def end(self):
+        for k in range(1, DEPTH):
+            self.copy(Z, 0, k).wait_send()
+        for k in range(DEPTH):
+            self.copy(X, 0, k).wait_send()
+            self.copy(Y, 0, k).wait_send()
+            self.copy(ACROSS, 1 if k in Y_PATH else 2, k).wait_send()
+            for r in range(COLS):
+                self.copy(PAIR, r, k).wait_send()
+
+
+def place_vectors(place, vectors, out):
+    out[...] = jnp.zeros_like(out)
+    for ref, row in zip(vectors, (LN1G, LN1B, QB, PROJB, LN2G, LN2B, OUTB, FCB)):
+        size = ref.shape[1]
+        start = place.index * size
+        at_row, at_lane = lax.div(start, D), lax.rem(start, D)
+        lane = lax.broadcasted_iota(jnp.int32, (size, D), 1)
+        pick = lax.broadcasted_iota(jnp.int32, (size, D), 0) + at_lane == lane
+        values = dot(ref[...], jnp.where(pick, 1.0, 0.0).astype(BF16))
+        rows = (size * 32) // D
+        mine = lax.broadcasted_iota(jnp.int32, (rows, D), 0) == at_row
+        out[row : row + rows, :] = jnp.where(mine, values, 0.0)
+
+
+SUM_STEPS = 6
+
+
+class TableSum:
+    def __init__(self, place, total, got, send, recv):
+        self.place, self.total, self.got, self.send, self.recv = place, total, got, send, recv
+
+    def copy(self, step, arriving=False):
+        place = self.place
+        if step == 0:
+            device, n = place.partner, 0
+        elif step <= 3:
+            device, n = place.along[step], (step if arriving else 4 - step)
+        else:
+            device, n = (place.x, place.y)[step - 4], step
+        stage = 0 if step == 0 else (1 if step <= 3 else step - 2)
+        return remote(self.total.at[stage], self.got.at[n], self.send.at[step], self.recv.at[n], device)
+
+    def begin(self, steps):
+        for step in steps:
+            self.copy(step).start()
+
+    def add(self, stage, steps):
+        for step in steps:
+            self.copy(step, True).wait_recv()
+        total = self.total[stage]
+        for step in steps:
+            total = total + self.got[step]
+        self.total[stage + 1] = total
+
+    def end(self):
+        for step in range(SUM_STEPS):
+            self.copy(step).wait_send()
+
+
+def forward_gather_kernel(
+    ssplit,
+    lsplit,
+    xs_hbm,
+    xl_hbm,
+    wqkv,
+    wproj,
+    wfc,
+    wout,
+    v0,
+    v1,
+    v2,
+    v3,
+    v4,
+    v5,
+    v6,
+    v7,
+    table_ref,
+    wa_hbm,
+    wf_hbm,
+    wo_hbm,
+    a1_hbm,
+    qkv_hbm,
+    att_hbm,
+    lse_t_ref,
+    mid_hbm,
+    xs,
+    xl,
+    wa,
+    a1_ref,
+    qkv_ref,
+    att_ref,
+    mid_ref,
+    lse_ref,
+    slab_f,
+    swap_out,
+    swap_in,
+    total,
+    got,
+    io_sem,
+    swap_send,
+    swap_recv,
+    sum_send,
+    sum_recv,
+    g_send,
+    g_recv,
+):
+    place = Place()
+    loads = [pltpu.make_async_copy(xs_hbm, xs, io_sem.at[0]), pltpu.make_async_copy(xl_hbm, xl, io_sem.at[1])]
+    for copy in loads:
+        copy.start()
+    place_vectors(place, (v0, v1, v2, v3, v4, v5, v6, v7), total.at[0])
+    half = wa.shape[1] // 2
+    mine, theirs = place.core * half, (1 - place.core) * half
+    n_qkv = wqkv.shape[1]
+    a_share = jnp.concatenate([wqkv[...], wproj[...]], axis=1).astype(F32)
+    f_share = wfc[...].astype(F32)
+    first = place.core == 0
+    keep = []
+    for n, share in enumerate((a_share, f_share)):
+        left, right = share[:, 0:half], share[:, half : 2 * half]
+        swap_out[n] = jnp.where(first, right, left)
+        keep.append(jnp.where(first, left, right))
+    place.greet()
+    swaps = [
+        remote(swap_out.at[n], swap_in.at[n], swap_send.at[n], swap_recv.at[n], place.partner)
+        for n in range(2)
+    ]
+    sums = TableSum(place, total, got, sum_send, sum_recv)
+    swaps[0].start()
+    sums.begin((0,))
+    swaps[1].start()
+
+    def joined(n):
+        swaps[n].wait_recv()
+        other = swap_in[n]
+        top, bottom = jnp.where(first, keep[n], other), jnp.where(first, other, keep[n])
+        return jnp.concatenate([top, bottom], axis=0).astype(BF16)
+
+    chip = place.col[0] * DEPTH + place.depth[0]
+    spot = (at(chip * 48, 48, 16), at(mine, half, 128))
+    wa[spot] = joined(0)
+    ga = Gather(place, wa, wa.at[spot], True, g_send.at[0], g_recv.at[0])
+    ga.begin()
+    sums.add(0, (0,))
+    sums.begin((1, 2, 3))
+    slab_f[...] = joined(1)
+    gf = Gather(place, wf_hbm, slab_f, True, g_send.at[1], g_recv.at[1])
+    go = Gather(place, wo_hbm, wout, False, g_send.at[2], g_recv.at[2])
+    own_f = pltpu.make_async_copy(slab_f, gf.spots[0, 0, 0], io_sem.at[2])
+    own_o = pltpu.make_async_copy(wout, go.spots[0, 0, 0], io_sem.at[3])
+    own_f.start()
+    own_o.start()
+    sums.add(1, (1, 2, 3))
+    sums.begin((4,))
+    ga.along(1)
+    sums.add(2, (4,))
+    sums.begin((5,))
+    ga.along(3)
+    sums.add(3, (5,))
+    table_ref[...] = total[4]
+    ga.along(2)
+    for copy in loads:
+        copy.wait()
+    groups = group_refs(xs, xl)
+    loop(groups[0][0].shape[0] // TILE, lambda t: norm_tile(xs, table_ref, a1_ref, 0, t))
+    ga.across(0)
+    gf.begin()
+    loop(2, lambda t: norm_tile(xl, table_ref, a1_ref, groups[1][1], t))
+    ga.across(1)
+    ga.across(3)
+    loop(xl.shape[0] // TILE - 2, lambda t: norm_tile(xl, table_ref, a1_ref, groups[1][1], t + 2))
+    ga.across(2)
+    go.begin()
+    for k in range(DEPTH):
+        ga.last(k)
+    ga.arrive()
+    stores = [
+        pltpu.make_async_copy(src, dst, io_sem.at[4 + n])
+        for n, (src, dst) in enumerate(
+            (
+                (wa, wa_hbm),
+                (a1_ref, a1_hbm),
+                (qkv_ref, qkv_hbm),
+                (att_ref, att_hbm),
+                (mid_ref, mid_hbm),
+            )
+        )
+    ]
+    stores[0].start()
+    stores[1].start()
+
+    def hooks(table):
+        def run(i):
+            for n, actions in table.items():
+
+                @pl.when(i == n)
+                def _():
+                    for action, k in actions:
+                        action(k)
+
+        return run
+
+    after = hooks(
+        {
+            0: ((gf.along, 1),),
+            1: ((gf.along, 3),),
+            2: ((gf.along, 2),),
+            3: ((go.along, 1),),
+            4: ((go.along, 3),),
+            5: ((go.along, 2), (gf.across, 0)),
+        }
+    )
+
+    def qkv_step(t):
+        qkv_tile(table_ref, wa, a1_ref, qkv_ref, t)
+        after(t)
+
+    loop(a1_ref.shape[0] // TILE, qkv_step)
+    stores[2].start()
+    lse_ref[...] = jnp.zeros_like(lse_ref)
+    after_short = hooks(
+        {
+            0: ((gf.across, 1),),
+            1: ((gf.across, 2),),
+            2: ((go.across, 1), (gf.last, 0)),
+            3: ((go.across, 2), (gf.last, 3)),
+            4: ((go.last, 0),),
+            5: ((go.last, 1),),
+        }
+    )
+    after_long = hooks(
+        {
+            0: ((gf.across, 3),),
+            1: ((go.across, 0), (gf.last, 1)),
+            2: ((go.across, 3), (gf.last, 2)),
+            4: ((go.last, 3),),
+            5: ((go.last, 2),),
+        }
+    )
+
+    def pair_step(pair):
+        attend_pair(ssplit[0], qkv_ref, att_ref, lse_ref, 0, xs.shape[0], pair)
+        after_short(pair)
+        attend_pair(lsplit[0], qkv_ref, att_ref, lse_ref, xs.shape[0], xl.shape[0], pair)
+        after_long(pair)
+
+    loop(PAIRS, pair_step)
+    stores[3].start()
+    lse_t_ref[...] = jnp.transpose(lse_ref[...])[:16, :]
+    for x_ref, base in groups:
+        loop(
+            x_ref.shape[0] // TILE,
+            lambda t: mid_tile(x_ref, table_ref, wa, att_ref, mid_ref, base, t),
+        )
+    stores[4].start()
+    gf.arrive()
+    go.arrive()
+    own_f.wait()
+    own_o.wait()
+    for swap in swaps:
+        swap.wait_send()
+    sums.end()
+    for g in (ga, gf, go):
+        g.end()
+    for copy in stores:
+        copy.wait()
+
+
+ANY = pl.BlockSpec(memory_space=pl.ANY)
+
+
+def forward_gather(ssplit, lsplit, xs, xl, wqkv, wproj, wfc, wout, vectors):
+    rows = xs.shape[0] + xl.shape[0]
+    devices = 2 * COLS * DEPTH
+    wide = wqkv.shape[1] + wproj.shape[1]
+    full_out = jax.ShapeDtypeStruct((wout.shape[0] * devices, wout.shape[1]), BF16)
+    sem = pltpu.SemaphoreType.DMA
+    return pl.pallas_call(
+        forward_gather_kernel,
+        out_shape=(
+            jax.ShapeDtypeStruct((16, D), F32),
+            jax.ShapeDtypeStruct((D, wide), BF16),
+            jax.ShapeDtypeStruct((D, wfc.shape[1]), BF16),
+            full_out,
+            jax.ShapeDtypeStruct((rows, D), BF16),
+            jax.ShapeDtypeStruct((rows, 3 * D), BF16),
+            jax.ShapeDtypeStruct((rows, D), BF16),
+            jax.ShapeDtypeStruct((16, rows), F32),
+            jax.ShapeDtypeStruct((rows, D), F32),
+        ),
+        in_specs=[SM, SM, ANY, ANY] + [VM] * 12,
+        out_specs=[VM, ANY, ANY, ANY, ANY, ANY, ANY, VM, ANY],
+        scratch_shapes=[
+            pltpu.VMEM(xs.shape, BF16),
+            pltpu.VMEM(xl.shape, BF16),
+            pltpu.VMEM((D, wide), BF16),
+            pltpu.VMEM((rows, D), BF16),
+            pltpu.VMEM((rows, 3 * D), BF16),
+            pltpu.VMEM((rows, D), BF16),
+            pltpu.VMEM((rows, D), F32),
+            pltpu.VMEM((rows, 128), F32),
+            pltpu.VMEM((48, wfc.shape[1] // 2), BF16),
+            pltpu.VMEM((2, 24, wide // 2), F32),
+            pltpu.VMEM((2, 24, wide // 2), F32),
+            pltpu.VMEM((5, 16, D), F32),
+            pltpu.VMEM((SUM_STEPS, 16, D), F32),
+            sem((9,)),
+            sem((2,)),
+            sem((2,)),
+            sem((SUM_STEPS,)),
+            sem((SUM_STEPS,)),
+            sem((3, N_GATHER)),
+            sem((3, N_GATHER)),
+        ],
+        compiler_params=pltpu.CompilerParams(
+            vmem_limit_bytes=VMEM_LIMIT, collective_id=0, has_side_effects=True
+        ),
+        name="attention_forward_gather",
+    )(ssplit, lsplit, xs, xl, wqkv, wproj, wfc, wout, *[v.reshape(1, -1) for v in vectors])
+
+
 AXES = ("dp", "fsdp")
 
 
@@ -516,6 +952,11 @@
     gxs, gxl, dwp, dwq, sums1 = backward_local(
         ss, ls, xs, xl, table, w_attn, a1, qkv, att, lse_t, g_mid
     )
+    return finish(args, devices, starts, sizes, out_s, out_l, gxs, gxl, sums1, sums2, dwq, dwp, dwf, dwo)
+
+
+def finish(args, devices, starts, sizes, out_s, out_l, gxs, gxl, sums1, sums2, dwq, dwp, dwf, dwo):
+    st, lt = args[0], args[1]
     rs = lambda x: x.reshape(devices, -1)
     small = jnp.concatenate(
         [
@@ -553,7 +994,27 @@
     )
 
 
-def per_device(devices, *args):
+def on_torus(args, devices):
+    (st, lt, ss, ls, ln1g, ln1b, wqkv, qvb, wproj, projb, ln2g, ln2b, wfc, fcb, wout, outb, sc, lc) = args
+    xs, xl = st.reshape(-1, D), lt.reshape(-1, D)
+    cs, cl = sc.reshape(-1, D), lc.reshape(-1, D)
+    vectors = (ln1g, ln1b, qvb, projb, ln2g, ln2b, outb, fcb)
+    sizes = [v.shape[0] for v in vectors]
+    starts = [sum(sizes[:i]) for i in range(len(sizes))]
+    table, w_attn, w_fc, w_out, a1, qkv, att, lse_t, mid = forward_gather(
+        ss, ls, xs, xl, wqkv, wproj, wfc, wout, vectors
+    )
+    out_s, out_l, g_mid, sums2, dwf, dwo = mlp_local(mid, cs, cl, table, w_fc, w_out, False)
+    gxs, gxl, dwp, dwq, sums1 = backward_local(
+        ss, ls, xs, xl, table, w_attn, a1, qkv, att, lse_t, g_mid
+    )
+    return finish(args, devices, starts, sizes, out_s, out_l, gxs, gxl, sums1, sums2, dwq, dwp, dwf, dwo)
+
+
+def per_device(shape, *args):
+    devices = shape["dp"] * shape["fsdp"]
+    if shape == {"dp": COLS, "fsdp": 2 * DEPTH}:
+        return on_torus(args, devices)
     return general(args, devices)
 
 
@@ -562,7 +1023,7 @@
     in_specs = (seq, seq, vec, vec) + (vec, vec, mat, vec, mat, vec) * 1 + (vec, vec, mat, vec, mat, vec) + (seq, seq)
     out_specs = (seq,) * 4 + (vec, vec, mat, vec, mat, vec) * 2
     return jax.shard_map(
-        functools.partial(per_device, mesh.size),
+        functools.partial(per_device, dict(mesh.shape)),
         mesh=mesh,
         in_specs=in_specs,
         out_specs=out_specs,

time: 883 us -> 791 us (0.90)
  waiting for transfers between devices: 558 us -> 463 us
  Pallas kernels: 207 us -> 260 us
  blocking collectives: 82.4 us -> 42.2 us
    all_gather x3 -> x0, waiting for transfers between devices: 93.5 us -> none  [gather(): return lax.all_gather(x, AXES, axis=axis, tiled=True)]
    pallas_call x1, Pallas kernels: 54.2 us -> 107 us  [forward_gather(): pl.pallas_call(forward_gather_kernel, out_shape=(jax.ShapeDtypeStruct((16...]
    unnamed x2 -> x1, blocking collectives: 82.4 us -> 42.2 us
  transfers between devices with their start and end apart: 7 -> 4, of which waited for: 7 -> 4; matrix products, arithmetic and copies ran while one was open for 1% -> 0% of each run, Pallas kernels for 6% -> 0%
where the time goes in v2:
time: 791 us; the launch traced here: 784 us
  waiting for transfers between devices  463 us (59%)
  Pallas kernels  260 us (33%)
  blocking collectives  42.2 us (5%)
  between operations  15.4 us (2%)
    reduce_scatter x4, waiting for transfers between devices, scatter(): return lax.psum_scatter(x, AXES, scatter_dimension=0, tiled=True)  461 us
    pallas_call x1, Pallas kernels, forward_gather(): pl.pallas_call(forward_gather_kernel, out_shape=(jax.ShapeDtypeStruct((16...  107 us
    pallas_call x1, Pallas kernels, mlp_local(): pl.pallas_call(functools.partial(mlp_kernel, (ns, nl), slabs), grid=(step...  80.8 us
    pallas_call x1, Pallas kernels, backward_local(): pl.pallas_call(backward_kernel, out_shape=(jax.ShapeDtypeStruct(xs.shape,...  72.2 us
    unnamed x1, blocking collectives  42.2 us
  transfers between devices with their start and end apart: 4, of which 4 were waited for; matrix products, arithmetic and copies ran while one was open for 0% of the time, Pallas kernels for 0%

profile of v2, /device:TPU:0, one launch (start us, length us, event | category | flops | bytes accessed | tf_op | source)
XLA Modules:
  0.0 784.2 jit_solution(16899930370906426235)
XLA Ops:
  7.2 0.0 reduce-scatter.7.cloned.1.call-start
  8.5 107.4 %attention_forward_gather.1 = (f32[16,768]{1,0:T(8,128)}, bf16[768,3072]{1,0:T(8,128)(2,1)}, bf16[768,3072]{1,0:T(8,128)(2,1)}, bf16[3072,768]{1,0:T(8,128)(2,1)...) custom-call(s32[1]{0:T(128)S(6)} %copy.34.ssplit, ...), custom_call_target="tpu_custom_call" | custom-call | tf_op jit(solution)/shard_map/attention_forward_gather/pallas_call | solution.py:883
  115.9 80.8 %mlp.1 = (bf16[512,768]{1,0:T(8,128)(2,1)}, bf16[1024,768]{1,0:T(8,128)(2,1)}, f32[1536,768]{1,0:T(8,128)}, f32[8,768]{1,0:T(8,128)}, f32[768,3072]{1,0:T(8,128)}, /*index=5*/f32[3072,768]{1,0:T(8,128)}) custom-call(f32[1536,768]{1,0:T(8,128)} %get-tuple-element.36.mid_ref, bf16[512,768]{1,0:T(8,128)(2,1)} %bitcast.37, bf16[1024,768]{1,0:T(8,128)(2,1)} %bitcast.36, ...), custom_call_target="tpu_custom_call" | custom-call | tf_op jit(solution)/shard_map/mlp/pallas_call | solution.py:308
  196.7 72.2 %attention_backward.1 = (f32[512,768]{1,0:T(8,128)}, f32[1024,768]{1,0:T(8,128)}, f32[768,768]{1,0:T(8,128)}, f32[768,2304]{1,0:T(8,128)}, f32[8,768]{1,0:T(8,128)}) custom-call(s32[1]{0:T(128)S(6)} %copy.34.ssplit, s32[1]{0:T(128)S(6)} %copy.35.lsplit, bf16[512,768]{1,0:T(8,128)(2,1)} %bitcast.35, bf16[1024,768]{1,0:T(8,128)(2,1)} %bitcast.33, ...), custom_call_target="tpu_custom_call" | custom-call | tf_op jit(solution)/shard_map/attention_backward/pallas_call | solution.py:472
  268.9 0.0 reduce-scatter.7.cloned.1.call-update
  268.9 0.0 reduce-scatter.5.cloned.1.call-start
  268.9 0.7 reduce-scatter.5.cloned.1.call-update
  269.6 0.0 reduce-scatter.11.cloned.1.call-start
  269.7 0.7 reduce-scatter.11.cloned.1.call-update
  270.4 0.0 reduce-scatter.9.cloned.1.call-start
  270.4 0.0 copy-start.1
  270.4 0.0 copy-start
  270.4 0.5 reduce-scatter.9.cloned.1.call-update
  270.9 0.2 copy-done.1
  271.2 0.1 reshape_squeeze.18
  271.3 0.1 reshape_squeeze.19
  271.4 0.1 reshape_squeeze.20
  271.4 0.1 reshape.110
  271.5 0.0 copy-done
  271.6 0.1 reshape_squeeze.21
  271.7 0.1 reshape_squeeze.22
  271.8 0.1 reshape_squeeze.23
  271.8 0.1 reshape.111
  271.9 0.1 concatenate.3
  272.0 42.2 %all-reduce = f32[32,288]{1,0:T(8,128)S(1)} all-reduce(f32[32,288]{1,0:T(8,128)S(1)} %concatenate.3), channel_id=2, replica_groups=mesh['dp'=4,'fsdp'=8] {'dp','fsdp'}, use_global_device_ids=true, to_apply=%region_0.0.clone | all-reduce | flops 9216 | bytes 73728
  314.2 0.6 dynamic-slice_bitcast_fusion.1
  314.8 0.6 dynamic-slice_bitcast_fusion.5
  315.4 0.6 dynamic-slice_bitcast_fusion
  316.0 52.8 %reduce-scatter.7.cloned.1.call-done = f32[24,768]{1,0:T(8,128)} async-done(((f32[768,768]{1,0:T(8,128)}), f32[24,768]{1,0:T(8,128)}) %reduce-scatter.7.cloned.1.call-update) | async-done | bytes 73744 | tf_op jit(solution)/shard_map/reduce_scatter | solution.py:935
  368.8 125.2 %reduce-scatter.5.cloned.1.call-done = f32[24,2304]{1,0:T(8,128)} async-done(((f32[768,2304]{1,0:T(8,128)}), f32[24,2304]{1,0:T(8,128)}) %reduce-scatter.5.cloned.1.call-update) | async-done | bytes 221200 | tf_op jit(solution)/shard_map/reduce_scatter | solution.py:935
  494.0 141.5 %reduce-scatter.11.cloned.1.call-done = f32[96,768]{1,0:T(8,128)} async-done(((f32[3072,768]{1,0:T(8,128)}), f32[96,768]{1,0:T(8,128)}) %reduce-scatter.11.cloned.1.call-update) | async-done | bytes 294928 | tf_op jit(solution)/shard_map/reduce_scatter | solution.py:935
  635.5 142.0 %reduce-scatter.9.cloned.1.call-done = f32[24,3072]{1,0:T(8,128)} async-done(((f32[768,3072]{1,0:T(8,128)}), f32[24,3072]{1,0:T(8,128)}) %reduce-scatter.9.cloned.1.call-update) | async-done | bytes 294928 | tf_op jit(solution)/shard_map/reduce_scatter | solution.py:935
  (4 shorter events, 0.1 us)
Async XLA Ops:
  7.2 361.6 %reduce-scatter.7.cloned.1.call-start = ((), (), s32[]{:S(2)}) async-start(), calls=%async_computation.5 | async-start | bytes 2433024 | tf_op jit(solution)/shard_map/reduce_scatter | solution.py:935
  268.9 225.1 %reduce-scatter.5.cloned.1.call-start = ((), (), s32[]{:S(2)}) async-start(), calls=%async_computation.4 | async-start | bytes 7299072 | tf_op jit(solution)/shard_map/reduce_scatter | solution.py:935
  269.6 365.8 %reduce-scatter.11.cloned.1.call-start = ((), (), s32[]{:S(2)}) async-start(), calls=%async_computation.7 | async-start | bytes 9732096 | tf_op jit(solution)/shard_map/reduce_scatter | solution.py:935
  270.4 507.1 %reduce-scatter.9.cloned.1.call-start = ((), (), s32[]{:S(2)}) async-start(), calls=%async_computation.6 | async-start | bytes 9732096 | tf_op jit(solution)/shard_map/reduce_scatter | solution.py:935
  270.4 0.7 copy-start.1
  270.4 1.1 copy-start
Sparse Core Ops, SparseCore 0:
  269.0 99.7 reduce-scatter.6
  376.0 117.9 reduce-scatter.4
  500.5 134.9 reduce-scatter.10
  642.8 134.6 reduce-scatter.8
